TPU v7x, 32 devices: a whole 2x2x4 slice. The times are simulated.
32 devices in a mesh: dp: 4 (over x, core), ctx: 2 (over y), tensor: 4 (over z).
Axes of the slice: x: 2, y: 2, z: 4, core: 2. Of those that a mesh axis runs over, the one named last changes fastest.
Arguments:
- block_input: bfloat16 [4, 4096, 768], P('dp', 'ctx'), may hold values from -6 to 6
- cotangent: bfloat16 [4, 4096, 768], P('dp', 'ctx'), may hold values from -6 to 6
- norm1_gain: bfloat16 [768], P('dp'), may hold values from 0.25 to 1.75
- norm1_bias: bfloat16 [768], P('dp'), may hold values from -1.5 to 1.5
- qkv_weight: bfloat16 [768, 3, 768], P('dp', None, 'tensor'), may hold values from -0.21875 to 0.21875
- qkv_bias: bfloat16 [2, 12, 64], P(None, 'tensor', 'dp'), may hold values from -1.5 to 1.5
- rel_pos_h: bfloat16 [127, 64], P(None, 'dp'), may hold values from -0.75 to 0.75
- rel_pos_w: bfloat16 [127, 64], P(None, 'dp'), may hold values from -0.75 to 0.75
- proj_weight: bfloat16 [768, 768], P('tensor', 'dp'), may hold values from -3 to 3
- proj_bias: bfloat16 [768], P('dp'), may hold values from -1.5 to 1.5
- norm2_gain: bfloat16 [768], P('dp'), may hold values from 0.25 to 1.75
- norm2_bias: bfloat16 [768], P('dp'), may hold values from -1.5 to 1.5
- mlp_in_weight: bfloat16 [768, 3072], P('dp', 'tensor'), may hold values from -0.21875 to 0.21875
- mlp_in_bias: bfloat16 [48, 64], P('tensor', 'dp'), may hold values from -2 to 2
- mlp_out_weight: bfloat16 [3072, 768], P('tensor', 'dp'), may hold values from -0.15625 to 0.15625
- mlp_out_bias: bfloat16 [768], P('dp'), may hold values from -1.5 to 1.5
Outputs:
- block_out: bfloat16 [4, 4096, 768], P('dp', 'ctx')
- grad_input: float32 [4, 4096, 768], P('dp', 'ctx')
- grad_norm1_gain: float32 [768], P('dp')
- grad_norm1_bias: float32 [768], P('dp')
- grad_qkv_weight: float32 [768, 3, 768], P('dp', None, 'tensor')
- grad_qkv_bias: float32 [2, 12, 64], P(None, 'tensor', 'dp')
- grad_rel_pos_h: float32 [127, 64], P(None, 'dp')
- grad_rel_pos_w: float32 [127, 64], P(None, 'dp')
- grad_proj_weight: float32 [768, 768], P('tensor', 'dp')
- grad_proj_bias: float32 [768], P('dp')
- grad_norm2_gain: float32 [768], P('dp')
- grad_norm2_bias: float32 [768], P('dp')
- grad_mlp_in_weight: float32 [768, 3072], P('dp', 'tensor')
- grad_mlp_in_bias: float32 [48, 64], P('tensor', 'dp')
- grad_mlp_out_weight: float32 [3072, 768], P('tensor', 'dp')
- grad_mlp_out_bias: float32 [768], P('dp')
All inputs are finite; a program needn't handle non-finite values.
Results may differ from a plain program's by a relative error of at most 0.023.
Values may be sent and summed in bfloat16 or wider, within the bound.
No kernel may reach another device: no remote copies, remote signals or barrier semaphores. Data moves between devices by JAX's collectives and lax.ppermute only.
A program may use at most 384 MiB of HBM per device.

v0:
```python
import jax
import jax.numpy as jnp
from jax import lax
from jax.sharding import PartitionSpec as P

HD = 64
GH = 64
GW = 64


norm_epsilon = 1e-06
score_scale = 0.125


def shifted(value, axis, steps):
    count = lax.axis_size(axis)
    pairs = [(source, (source + steps) % count) for source in range(count)]
    return lax.ppermute(value, axis, pairs)


def layer_norm(values, norm_gain, norm_shift):
    center = jnp.mean(values, axis=-1, keepdims=True)
    offset = values - center
    spread = jnp.mean(offset * offset, axis=-1, keepdims=True)
    return offset * lax.rsqrt(spread + norm_epsilon) * norm_gain + norm_shift


def smooth_gate(values):
    return jax.nn.gelu(values, approximate=False)


def gather_weights(shards):
    return (
        lax.all_gather(shards[0], "dp", axis=0, tiled=True),
        lax.all_gather(shards[1], "dp", axis=0, tiled=True),
        lax.all_gather(shards[2], "dp", axis=0, tiled=True),
        lax.all_gather(shards[3], "dp", axis=2, tiled=True),
        lax.all_gather(shards[4], "dp", axis=1, tiled=True),
        lax.all_gather(shards[5], "dp", axis=1, tiled=True),
        lax.all_gather(shards[6], "dp", axis=1, tiled=True),
        lax.all_gather(shards[7], "dp", axis=0, tiled=True),
        lax.all_gather(shards[8], "dp", axis=0, tiled=True),
        lax.all_gather(shards[9], "dp", axis=0, tiled=True),
        lax.all_gather(shards[10], "dp", axis=0, tiled=True),
        lax.all_gather(shards[11], "dp", axis=1, tiled=True),
        lax.all_gather(shards[12], "dp", axis=1, tiled=True),
        lax.all_gather(shards[13], "dp", axis=0, tiled=True),
    )


def head_total(pieces):
    return lax.psum(pieces.astype(jnp.bfloat16), "tensor").astype(jnp.float32)


def pass_keys(held_block):
    return shifted(held_block, "ctx", 1)


def pass_pairs(held_block):
    return shifted(held_block, "ctx", 1)


def pass_grads(held_block):
    return shifted(held_block.astype(jnp.bfloat16), "ctx", 1).astype(held_block.dtype)


def row_tables(table_h, table_w, first_row, rows_dev):
    rows_here = first_row + jnp.arange(rows_dev, dtype=jnp.int32)
    grid_rows = jnp.arange(GH, dtype=jnp.int32)
    spots_h = rows_here[:, None] - grid_rows[None, :] + (GH - 1)
    pick_h = (spots_h[:, :, None] == jnp.arange(2 * GH - 1, dtype=jnp.int32)[None, None, :]).astype(
        jnp.bfloat16
    )
    grid_cols = jnp.arange(GW, dtype=jnp.int32)
    spots_w = grid_cols[:, None] - grid_cols[None, :] + (GW - 1)
    pick_w = (spots_w[:, :, None] == jnp.arange(2 * GW - 1, dtype=jnp.int32)[None, None, :]).astype(
        jnp.bfloat16
    )
    chosen_h = jnp.einsum(
        "irt,tc->irc", pick_h, table_h, preferred_element_type=jnp.float32
    ).astype(jnp.bfloat16)
    chosen_w = jnp.einsum(
        "wst,tc->wsc", pick_w, table_w, preferred_element_type=jnp.float32
    ).astype(jnp.bfloat16)
    return (pick_h, pick_w, chosen_h, chosen_w)


def score_block(query4, key_part, near_h, far_w, source, rows_dev):
    images, tok_dev, heads_here, head_size = query4.shape
    key4 = key_part.reshape(images, tok_dev, heads_here, head_size)
    scores = (
        jnp.einsum("bnhc,bmhc->bhnm", query4, key4, preferred_element_type=jnp.float32)
        * score_scale
    )
    picked = lax.dynamic_slice_in_dim(near_h, source * rows_dev, rows_dev, 3)
    offset = (picked[:, :, :, :, None] + far_w[:, :, :, None, :]).reshape(scores.shape)
    return scores + offset


def log_normalizer(query4, key_flat, near_h, far_w, position, devices, rows_dev):

    def update(state, held_block, source):
        row_top, row_total = state
        scores = score_block(query4, held_block, near_h, far_w, source, rows_dev)
        new_top = jnp.maximum(row_top, jnp.max(scores, axis=-1))
        row_total = row_total * jnp.exp(row_top - new_top) + jnp.sum(
            jnp.exp(scores - new_top[..., None]), axis=-1
        )
        return (new_top, row_total)

    first_scores = score_block(query4, key_flat, near_h, far_w, position, rows_dev)
    first_top = jnp.max(first_scores, axis=-1)
    start_state = (first_top, jnp.sum(jnp.exp(first_scores - first_top[..., None]), axis=-1))

    def turn(turn_index, carry):
        held_block, state = carry
        source = (position - turn_index) % devices
        held_block = pass_keys(held_block)
        return (held_block, update(state, held_block, source))

    row_top, row_total = lax.fori_loop(1, devices, turn, (key_flat, start_state))[1]
    return row_top + jnp.log(row_total)


def attend(query4, pairs, log_norm, near_h, far_w, position, devices, rows_dev, precise):
    images, tok_dev, heads_here, head_size = query4.shape
    head_width = heads_here * head_size

    def contribute(totals, held_block, source):
        scores = score_block(query4, held_block[:, :, :head_width], near_h, far_w, source, rows_dev)
        weights = jnp.exp(scores - log_norm[..., None])
        value4 = held_block[:, :, head_width:].reshape(images, tok_dev, heads_here, head_size)
        rounded = weights.astype(jnp.bfloat16)
        low_term = jnp.einsum(
            "bhnm,bmhc->bnhc", rounded, value4, preferred_element_type=jnp.float32
        )
        low_sum = totals[0] + low_term
        if precise:
            rest = (weights - rounded.astype(jnp.float32)).astype(jnp.bfloat16)
            high_sum = (
                totals[1]
                + low_term
                + jnp.einsum("bhnm,bmhc->bnhc", rest, value4, preferred_element_type=jnp.float32)
            )
            return (low_sum, high_sum)
        return (low_sum, totals[1])

    zeros_sum = jnp.zeros((images, tok_dev, heads_here, head_size), jnp.float32)
    totals = contribute((zeros_sum, zeros_sum), pairs, position)

    def turn(turn_index, carry):
        held_block, totals = carry
        source = (position - turn_index) % devices
        held_block = pass_pairs(held_block)
        return (held_block, contribute(totals, held_block, source))

    return lax.fori_loop(1, devices, turn, (pairs, totals))[1]


def attend_back(
    query4, pairs, log_norm, row_delta, grad_heads4, near_h, far_w, position, devices, rows_dev
):
    images, tok_dev, heads_here, head_size = query4.shape
    head_width = heads_here * head_size

    def contribute(carry, held_block, source):
        grad_query, grad_near, grad_far, grad_block = carry
        key4 = held_block[:, :, :head_width].reshape(images, tok_dev, heads_here, head_size)
        value4 = held_block[:, :, head_width:].reshape(images, tok_dev, heads_here, head_size)
        scores = score_block(query4, held_block[:, :, :head_width], near_h, far_w, source, rows_dev)
        weights = jnp.exp(scores - log_norm[..., None])
        grad_weights = jnp.einsum(
            "bnhc,bmhc->bhnm", grad_heads4, value4, preferred_element_type=jnp.float32
        )
        grad_scores = (weights * (grad_weights - row_delta[..., None])).astype(jnp.bfloat16)
        grad_query = (
            grad_query
            + jnp.einsum("bhnm,bmhc->bnhc", grad_scores, key4, preferred_element_type=jnp.float32)
            * score_scale
        )
        grid_sums = grad_scores.astype(jnp.float32).reshape(
            images, heads_here, tok_dev, rows_dev, GW
        )
        grad_near = lax.dynamic_update_slice_in_dim(
            grad_near, jnp.sum(grid_sums, axis=4), source * rows_dev, 3
        )
        grad_far = grad_far + jnp.sum(grid_sums, axis=3)
        grad_key = (
            jnp.einsum("bhnm,bnhc->bmhc", grad_scores, query4, preferred_element_type=jnp.float32)
            * score_scale
        )
        grad_value = jnp.einsum(
            "bhnm,bnhc->bmhc",
            weights.astype(jnp.bfloat16),
            grad_heads4,
            preferred_element_type=jnp.float32,
        )
        grad_block = grad_block + jnp.concatenate(
            [
                grad_key.reshape(images, tok_dev, head_width),
                grad_value.reshape(images, tok_dev, head_width),
            ],
            axis=-1,
        )
        return (grad_query, grad_near, grad_far, grad_block)

    start_carry = (
        jnp.zeros((images, tok_dev, heads_here, head_size), jnp.float32),
        jnp.zeros(near_h.shape, jnp.float32),
        jnp.zeros(far_w.shape, jnp.float32),
        jnp.zeros(pairs.shape, jnp.float32),
    )
    start_carry = contribute(start_carry, pairs, position)

    def turn(turn_index, state):
        held_block, carry = state
        source = (position - turn_index) % devices
        held_block = pass_pairs(held_block)
        grad_query, grad_near, grad_far, grad_block = carry
        grad_block = pass_grads(grad_block)
        carry = contribute((grad_query, grad_near, grad_far, grad_block), held_block, source)
        return (held_block, carry)

    grad_query, grad_near, grad_far, grad_block = lax.fori_loop(
        1, devices, turn, (pairs, start_carry)
    )[1]
    return (grad_query, grad_near, grad_far, pass_grads(grad_block))


def forward(block_input, weights, precise):
    (
        gain_one,
        shift_one,
        weight_qkv,
        bias_qkv,
        table_h,
        table_w,
        weight_proj,
        bias_proj,
        gain_two,
        shift_two,
        weight_in,
        bias_in,
        weight_out,
        bias_out,
    ) = weights
    images, tok_dev, model_width = block_input.shape
    heads_here = bias_qkv.shape[1]
    head_width = heads_here * HD
    rows_dev = tok_dev // GW
    devices = lax.axis_size("ctx")
    position = lax.axis_index("ctx")
    residual = block_input.astype(jnp.float32)
    normed = layer_norm(
        residual, gain_one.astype(jnp.float32), shift_one.astype(jnp.float32)
    ).astype(jnp.bfloat16)
    projected = jnp.einsum("bnd,dje->bnje", normed, weight_qkv, preferred_element_type=jnp.float32)
    bias_flat = bias_qkv.astype(jnp.float32).reshape(2, head_width)
    query = (projected[:, :, 0] + bias_flat[0]).astype(jnp.bfloat16)
    key_rows = projected[:, :, 1].astype(jnp.bfloat16)
    value_rows = (projected[:, :, 2] + bias_flat[1]).astype(jnp.bfloat16)
    pick_h, pick_w, chosen_h, chosen_w = row_tables(table_h, table_w, position * rows_dev, rows_dev)
    query_grid = query.reshape(images, rows_dev, GW, heads_here, HD)
    near_h = jnp.einsum(
        "biwhc,irc->bhiwr", query_grid, chosen_h, preferred_element_type=jnp.float32
    ).reshape(images, heads_here, tok_dev, GH)
    far_w = jnp.einsum(
        "biwhc,wsc->bhiws", query_grid, chosen_w, preferred_element_type=jnp.float32
    ).reshape(images, heads_here, tok_dev, GW)
    query4 = query.reshape(images, tok_dev, heads_here, HD)
    pairs = jnp.concatenate([key_rows, value_rows], axis=-1)
    log_norm = log_normalizer(
        query4,
        key_rows.reshape(images, tok_dev * head_width),
        near_h,
        far_w,
        position,
        devices,
        rows_dev,
    )
    low_sum, high_sum = attend(
        query4, pairs, log_norm, near_h, far_w, position, devices, rows_dev, precise
    )
    heads_out = low_sum.reshape(images, tok_dev, head_width).astype(jnp.bfloat16)
    branch = head_total(
        jnp.dot(heads_out, weight_proj, preferred_element_type=jnp.float32)
    ) + bias_proj.astype(jnp.float32)
    middle = residual + branch
    normed_two = layer_norm(
        middle, gain_two.astype(jnp.float32), shift_two.astype(jnp.float32)
    ).astype(jnp.bfloat16)
    hidden = jnp.dot(normed_two, weight_in, preferred_element_type=jnp.float32) + bias_in.astype(
        jnp.float32
    ).reshape(-1)
    active = smooth_gate(hidden).astype(jnp.bfloat16)
    result = middle + (
        head_total(jnp.dot(active, weight_out, preferred_element_type=jnp.float32))
        + bias_out.astype(jnp.float32)
    )
    return {
        "result": result,
        "weights": weights,
        "residual": residual,
        "normed": normed,
        "query_grid": query_grid,
        "query4": query4,
        "pairs": pairs,
        "collected": None,
        "log_norm": log_norm,
        "near_h": near_h,
        "far_w": far_w,
        "pick_h": pick_h,
        "pick_w": pick_w,
        "chosen_h": chosen_h,
        "chosen_w": chosen_w,
        "heads_out": heads_out,
        "high_sum": high_sum,
        "middle": middle,
        "normed_two": normed_two,
        "hidden": hidden,
        "active": active,
    }


def per_device(
    block_input,
    cotangent,
    norm1_gain,
    norm1_bias,
    qkv_weight,
    qkv_bias,
    rel_pos_h,
    rel_pos_w,
    proj_weight,
    proj_bias,
    norm2_gain,
    norm2_bias,
    mlp_in_weight,
    mlp_in_bias,
    mlp_out_weight,
    mlp_out_bias,
):
    shards = (
        norm1_gain,
        norm1_bias,
        qkv_weight,
        qkv_bias,
        rel_pos_h,
        rel_pos_w,
        proj_weight,
        proj_bias,
        norm2_gain,
        norm2_bias,
        mlp_in_weight,
        mlp_in_bias,
        mlp_out_weight,
        mlp_out_bias,
    )
    block_out = forward(block_input, gather_weights(shards), False)["result"]
    stored = forward(block_input, gather_weights(shards), True)
    (
        gain_one,
        shift_one,
        weight_qkv,
        bias_qkv,
        table_h,
        table_w,
        weight_proj,
        bias_proj,
        gain_two,
        shift_two,
        weight_in,
        bias_in,
        weight_out,
        bias_out,
    ) = stored["weights"]
    images, tok_dev, model_width = block_input.shape
    heads_here = bias_qkv.shape[1]
    head_width = heads_here * HD
    rows_dev = tok_dev // GW
    devices = lax.axis_size("ctx")
    position = lax.axis_index("ctx")
    grad_result = cotangent.astype(jnp.float32)
    grad_weight_out = jnp.einsum(
        "bnf,bnd->fd", stored["active"], cotangent, preferred_element_type=jnp.float32
    )
    grad_bias_out = jnp.sum(grad_result, axis=(0, 1))
    grad_active = jnp.einsum(
        "bnd,fd->bnf", cotangent, weight_out, preferred_element_type=jnp.float32
    )
    grad_hidden = jax.vjp(smooth_gate, stored["hidden"])[1](grad_active)[0].astype(jnp.bfloat16)
    grad_weight_in = jnp.einsum(
        "bnd,bnf->df", stored["normed_two"], grad_hidden, preferred_element_type=jnp.float32
    )
    grad_bias_in = jnp.sum(grad_hidden.astype(jnp.float32), axis=(0, 1)).reshape(bias_in.shape)
    grad_normed_two = lax.psum(
        jnp.einsum(
            "bnf,df->bnd", grad_hidden, weight_in, preferred_element_type=jnp.float32
        ).astype(jnp.bfloat16),
        "tensor",
    ).astype(jnp.float32)
    gain_two_f = gain_two.astype(jnp.float32)
    shift_two_f = shift_two.astype(jnp.float32)
    grad_mid_norm, grad_gain_two, grad_shift_two = jax.vjp(
        layer_norm, stored["middle"], gain_two_f, shift_two_f
    )[1](grad_normed_two)
    grad_middle = grad_result + grad_mid_norm
    grad_branch = grad_middle.astype(jnp.bfloat16)
    grad_weight_proj = jnp.einsum(
        "bnk,bnd->kd", stored["heads_out"], grad_branch, preferred_element_type=jnp.float32
    )
    grad_bias_proj = jnp.sum(grad_branch.astype(jnp.float32), axis=(0, 1))
    grad_heads = jnp.einsum(
        "bnd,kd->bnk", grad_branch, weight_proj, preferred_element_type=jnp.float32
    ).astype(jnp.bfloat16)
    grad_heads4 = grad_heads.reshape(images, tok_dev, heads_here, HD)
    row_delta = jnp.einsum(
        "bnhc,bnhc->bhn",
        grad_heads4.astype(jnp.float32),
        stored["high_sum"],
        precision=lax.Precision.HIGHEST,
    )
    grad_query, grad_near, grad_far, grad_block = attend_back(
        stored["query4"],
        stored["pairs"],
        stored["log_norm"],
        row_delta,
        grad_heads4,
        stored["near_h"],
        stored["far_w"],
        position,
        devices,
        rows_dev,
    )
    grad_near5 = grad_near.reshape(images, heads_here, rows_dev, GW, GH)
    grad_far5 = grad_far.reshape(images, heads_here, rows_dev, GW, GW)
    from_tables = jnp.einsum(
        "bhiwr,irc->biwhc",
        grad_near5,
        stored["chosen_h"].astype(jnp.float32),
        precision=lax.Precision.HIGHEST,
    ) + jnp.einsum(
        "bhiws,wsc->biwhc",
        grad_far5,
        stored["chosen_w"].astype(jnp.float32),
        precision=lax.Precision.HIGHEST,
    )
    grad_query = (grad_query + from_tables.reshape(images, tok_dev, heads_here, HD)).astype(
        jnp.bfloat16
    )
    grad_query = grad_query.reshape(images, tok_dev, head_width)
    query_float = stored["query_grid"].astype(jnp.float32)
    grad_chosen_h = jnp.einsum(
        "biwhc,bhiwr->irc", query_float, grad_near5, precision=lax.Precision.HIGHEST
    )
    grad_chosen_w = jnp.einsum(
        "biwhc,bhiws->wsc", query_float, grad_far5, precision=lax.Precision.HIGHEST
    )
    grad_table_h = jnp.einsum(
        "irt,irc->tc",
        stored["pick_h"].astype(jnp.float32),
        grad_chosen_h,
        precision=lax.Precision.HIGHEST,
    )
    grad_table_w = jnp.einsum(
        "wst,wsc->tc",
        stored["pick_w"].astype(jnp.float32),
        grad_chosen_w,
        precision=lax.Precision.HIGHEST,
    )
    grad_pairs = grad_block.astype(jnp.bfloat16)
    grad_value = grad_pairs[:, :, head_width:]
    grad_projected = jnp.stack([grad_query, grad_pairs[:, :, :head_width], grad_value], axis=2)
    grad_weight_qkv = jnp.einsum(
        "bnd,bnje->dje", stored["normed"], grad_projected, preferred_element_type=jnp.float32
    )
    grad_bias_qkv = jnp.stack(
        [
            jnp.sum(grad_query.astype(jnp.float32), axis=(0, 1)),
            jnp.sum(grad_value.astype(jnp.float32), axis=(0, 1)),
        ]
    ).reshape(2, heads_here, HD)
    grad_normed, grad_table_h, grad_table_w = (
        lax.psum(
            jnp.einsum(
                "bnje,dje->bnd", grad_projected, weight_qkv, preferred_element_type=jnp.float32
            ).astype(jnp.bfloat16),
            "tensor",
        ).astype(jnp.float32),
        lax.psum(grad_table_h.astype(jnp.bfloat16), "tensor").astype(jnp.float32),
        lax.psum(grad_table_w.astype(jnp.bfloat16), "tensor").astype(jnp.float32),
    )
    gain_one_f = gain_one.astype(jnp.float32)
    shift_one_f = shift_one.astype(jnp.float32)
    grad_in_norm, grad_gain_one, grad_shift_one = jax.vjp(
        layer_norm, stored["residual"], gain_one_f, shift_one_f
    )[1](grad_normed)
    grad_input = grad_middle + grad_in_norm
    owned = (
        lax.psum_scatter(
            grad_gain_one.astype(jnp.bfloat16), "dp", scatter_dimension=0, tiled=True
        ).astype(jnp.float32),
        lax.psum_scatter(
            grad_shift_one.astype(jnp.bfloat16), "dp", scatter_dimension=0, tiled=True
        ).astype(jnp.float32),
        lax.psum_scatter(
            grad_weight_qkv.astype(jnp.bfloat16), "dp", scatter_dimension=0, tiled=True
        ).astype(jnp.float32),
        lax.psum_scatter(
            grad_bias_qkv.astype(jnp.bfloat16), "dp", scatter_dimension=2, tiled=True
        ).astype(jnp.float32),
        lax.psum_scatter(
            grad_table_h.astype(jnp.bfloat16), "dp", scatter_dimension=1, tiled=True
        ).astype(jnp.float32),
        lax.psum_scatter(
            grad_table_w.astype(jnp.bfloat16), "dp", scatter_dimension=1, tiled=True
        ).astype(jnp.float32),
        lax.psum_scatter(
            grad_weight_proj.astype(jnp.bfloat16), "dp", scatter_dimension=1, tiled=True
        ).astype(jnp.float32),
        lax.psum_scatter(
            grad_bias_proj.astype(jnp.bfloat16), "dp", scatter_dimension=0, tiled=True
        ).astype(jnp.float32),
        lax.psum_scatter(
            grad_gain_two.astype(jnp.bfloat16), "dp", scatter_dimension=0, tiled=True
        ).astype(jnp.float32),
        lax.psum_scatter(
            grad_shift_two.astype(jnp.bfloat16), "dp", scatter_dimension=0, tiled=True
        ).astype(jnp.float32),
        lax.psum_scatter(
            grad_weight_in.astype(jnp.bfloat16), "dp", scatter_dimension=0, tiled=True
        ).astype(jnp.float32),
        lax.psum_scatter(
            grad_bias_in.astype(jnp.bfloat16), "dp", scatter_dimension=1, tiled=True
        ).astype(jnp.float32),
        lax.psum_scatter(
            grad_weight_out.astype(jnp.bfloat16), "dp", scatter_dimension=1, tiled=True
        ).astype(jnp.float32),
        lax.psum_scatter(
            grad_bias_out.astype(jnp.bfloat16), "dp", scatter_dimension=0, tiled=True
        ).astype(jnp.float32),
    )
    reduced = (
        lax.psum(owned[0].astype(jnp.bfloat16), "ctx").astype(jnp.float32),
        lax.psum(owned[1].astype(jnp.bfloat16), "ctx").astype(jnp.float32),
        lax.psum(owned[2].astype(jnp.bfloat16), "ctx").astype(jnp.float32),
        lax.psum(owned[3].astype(jnp.bfloat16), "ctx").astype(jnp.float32),
        lax.psum(owned[4].astype(jnp.bfloat16), "ctx").astype(jnp.float32),
        lax.psum(owned[5].astype(jnp.bfloat16), "ctx").astype(jnp.float32),
        lax.psum(owned[6].astype(jnp.bfloat16), "ctx").astype(jnp.float32),
        lax.psum(owned[7].astype(jnp.bfloat16), "ctx").astype(jnp.float32),
        lax.psum(owned[8].astype(jnp.bfloat16), "ctx").astype(jnp.float32),
        lax.psum(owned[9].astype(jnp.bfloat16), "ctx").astype(jnp.float32),
        lax.psum(owned[10].astype(jnp.bfloat16), "ctx").astype(jnp.float32),
        lax.psum(owned[11].astype(jnp.bfloat16), "ctx").astype(jnp.float32),
        lax.psum(owned[12].astype(jnp.bfloat16), "ctx").astype(jnp.float32),
        lax.psum(owned[13].astype(jnp.bfloat16), "ctx").astype(jnp.float32),
    )
    return (
        block_out.astype(jnp.bfloat16),
        grad_input,
        reduced[0],
        reduced[1],
        reduced[2],
        reduced[3],
        reduced[4],
        reduced[5],
        reduced[6],
        reduced[7],
        reduced[8],
        reduced[9],
        reduced[10],
        reduced[11],
        reduced[12],
        reduced[13],
    )


def solution(mesh):
    placed = (
        P("dp", "ctx", None),
        P("dp", "ctx", None),
        P("dp"),
        P("dp"),
        P("dp", None, "tensor"),
        P(None, "tensor", "dp"),
        P(None, "dp"),
        P(None, "dp"),
        P("tensor", "dp"),
        P("dp"),
        P("dp"),
        P("dp"),
        P("dp", "tensor"),
        P("tensor", "dp"),
        P("tensor", "dp"),
        P("dp"),
    )
    return jax.shard_map(
        per_device,
        mesh=mesh,
        in_specs=placed,
        out_specs=(
            P("dp", "ctx", None),
            P("dp", "ctx", None),
            P("dp"),
            P("dp"),
            P("dp", None, "tensor"),
            P(None, "tensor", "dp"),
            P(None, "dp"),
            P(None, "dp"),
            P("tensor", "dp"),
            P("dp"),
            P("dp"),
            P("dp"),
            P("dp", "tensor"),
            P("tensor", "dp"),
            P("tensor", "dp"),
            P("dp"),
        ),
        check_vma=False,
    )
```

profile of v0, /device:TPU:0, one launch (start us, length us, event | category | flops | bytes accessed | tf_op | source)
XLA Modules:
  0.0 1312.7 jit_solution(12438150989890927648)
XLA Ops:
  16.6 13.8 %all_gather.57 = bf16[768,3,192]{2,1,0:T(4,128)(2,1)} all-gather(bf16[192,3,192]{2,1,0:T(4,128)(2,1)S(1)} %copy.154), channel_id=1, replica_groups=mesh['dp'=4,'ctx'=2,'tensor'=4] {'dp'}, dimensions={0}, use_global_device_ids=true | all-gather | bytes 1105920 | tf_op jit(solution)/shard_map/all_gather | solution.py:36
  40.0 12.0 all-reduce.15
  111.8 33.0 %broadcast_add_fusion = (f32[3,2048,32,64]{1,3,2,0:T(8,128)}, f32[3,2048,32,64]{1,3,2,0:T(8,128)}) fusion(f32[3,2048,32]{1,2,0:T(8,128)S(1)} %get-tuple-element.279, f32[3,2048,64]{1,2,0:T(8,128)} %add.546, f32[3,2048,32]{1,2,0:T(8,128)S(1)} %get-tuple-element.280), kind=kLoop, calls=%fused_computation.18 | loop fusion | flops 25165824 | bytes 103809024 | tf_op jit(solution)/shard_map/while/body/eval_jaxpr/add | solution.py:96
  144.8 32.5 %fusion.143 = (f32[3,2048]{1,0:T(4,128)S(1)}, f32[3,2048,2048]{1,2,0:T(8,128)}) fusion(f32[3,2048,32,64]{1,3,2,0:T(8,128)} %get-tuple-element.278, bf16[2048,3,64]{0,2,1:T(8,128)(2,1)S(1)} %add_convert_fusion.5, bf16[2048,3,64]{0,2,1:T(8,128)(2,1)S(1)} %bitcast.299), kind=kOutput, calls=%fused_computation.195 | convolution fusion | flops 1648355328 | bytes 102260736 | tf_op jit(solution)/shard_map/bnhc,bmhc->bhnm/dot_general | solution.py:92
  185.0 17.5 %reduce.35 = bf16[393216]{0:T(1024)(128)(2,1)S(1)} reduce(bf16[1,393216]{1,0:T(2,128)(2,1)} %collective-permute-done, bf16[]{:T(256)} %constant.260), dimensions={0}, to_apply=%ppermute.20.reduce_sub_computation | reduce | bytes 1572866 | tf_op jit(solution)/shard_map/while/body/eval_jaxpr/ppermute | solution.py:18
  204.9 32.9 %fusion.5 = (f32[3,2048]{1,0:T(4,128)S(1)}, f32[3,2048,2048]{1,2,0:T(8,128)}) fusion(f32[3,2048,32,64]{1,3,2,0:T(8,128)} %get-tuple-element.277, bf16[2048,3,64]{0,2,1:T(8,128)(2,1)S(1)} %add_convert_fusion.5, bf16[2048,3,64]{2,1,0:T(4,128)(2,1)} %reshape.872), kind=kOutput, calls=%fused_computation.21 | convolution fusion | flops 1648355328 | bytes 102260736 | tf_op jit(solution)/shard_map/while/body/eval_jaxpr/bnhc,bmhc->bhnm/dot_general | solution.py:92
  237.9 46.8 %exponential_reduce_fusion = (f32[3,2048]{1,0:T(4,128)S(1)}, f32[3,2048]{1,0:T(4,128)S(1)}) fusion(f32[3,2048]{1,0:T(4,128)S(1)} %max.15, f32[3,2048,32,64]{1,3,2,0:T(8,128)} %get-tuple-element.277, f32[3,2048,2048]{1,2,0:T(8,128)} %get-tuple-element.288, f32[3,2048,2048]{1,2,0:T(8,128)} %get-tuple-element.286, f32[3,2048]{1,0:T(4,128)S(1)} %get-tuple-element.285), kind=kLoop, calls=%fused_computation.14 | loop fusion | flops 75485184 | bytes 151093248 | tf_op jit(solution)/shard_map/while/body/eval_jaxpr/reduce_sum | solution.py:106
  286.3 32.1 %fusion.1 = f32[3,2048,2048]{1,2,0:T(8,128)} fusion(f32[3,2048,32,64]{1,3,2,0:T(8,128)} %get-tuple-element.277, f32[3,2048]{1,0:T(4,128)S(1)} %log_add_fusion, bf16[2048,3,64]{0,2,1:T(8,128)(2,1)S(1)} %add_convert_fusion.5, bf16[2048,3,64]{0,2,1:T(8,128)(2,1)S(1)} %bitcast.301), kind=kOutput, calls=%fused_computation.7 | convolution fusion | flops 1648361472 | bytes 102260736 | tf_op jit(solution)/shard_map/while/body/eval_jaxpr/bnhc,bmhc->bhnm/dot_general | solution.py:92
  318.4 17.3 %convolution_bitcast_fusion = f32[1,2048,3,64]{1,3,2,0:T(8,128)S(1)} fusion(bf16[2048,3,64]{0,2,1:T(8,128)(2,1)S(1)} %bitcast.296, f32[3,2048,2048]{1,2,0:T(8,128)} %fusion.1), kind=kOutput, calls=%fused_computation.106 | convolution fusion | flops 1623195648 | bytes 52690944 | tf_op jit(solution)/shard_map/while/body/eval_jaxpr/bhnm,bmhc->bnhc/dot_general | solution.py:134
  335.8 19.6 %add_convert_fusion.4 = (bf16[1,2048,3,64]{1,3,2,0:T(8,128)(2,1)S(1)}, f32[1,2048,3,64]{1,3,2,0:T(8,128)}) fusion(f32[1,2048,3,64]{1,3,2,0:T(8,128)S(1)} %convolution_bitcast_fusion, bf16[2048,3,64]{0,2,1:T(8,128)(2,1)S(1)} %add_convert_fusion.6, f32[3,2048,2048]{1,2,0:T(8,128)} %get-tuple-element.286, f32[3,2048]{1,0:T(4,128)S(1)} %log_add_fusion), kind=kOutput, calls=%fused_computation.137 | convolution fusion | flops 1636564992 | bytes 55074816 | tf_op jit(solution)/shard_map/bhnm,bmhc->bnhc/dot_general | solution.py:134
  365.7 114.6 %all-reduce.23.cloned.1.call-done = bf16[1,2048,768]{2,1,0:T(8,128)(2,1)} async-done(((bf16[1,2048,768]{2,1,0:T(8,128)(2,1)}), bf16[1,2048,768]{2,1,0:T(8,128)(2,1)}) %all-reduce.23.cloned.1.call-update) | async-done | bytes 3145744 | tf_op jit(solution)/shard_map/psum | solution.py:52
  485.3 20.1 %multiply_convert_fusion.2 = (bf16[2048,768]{1,0:T(8,128)(2,1)}, f32[2048,768]{1,0:T(8,128)}, f32[2048,768]{1,0:T(8,128)}) fusion(f32[768]{0:T(1024)S(1)} %reshape.889, bf16[768,768]{1,0:T(8,128)(2,1)} %all-gather.3.cloned.1.call-done, f32[768]{0:T(1024)S(1)} %convert_element_type.413, f32[768]{0:T(1024)S(1)} %convert_element_type.412, ...), kind=kOutput, calls=%fused_computation.55 | convolution fusion | flops 2533883904 | bytes 23228416 | tf_op jit(solution)/shard_map/dot_general | solution.py:292
  505.4 11.1 fusion.145
  522.2 120.2 %all-reduce.25.cloned.1.call-done = bf16[1,2048,768]{2,1,0:T(8,128)(2,1)} async-done(((bf16[1,2048,768]{2,1,0:T(8,128)(2,1)}), bf16[1,2048,768]{2,1,0:T(8,128)(2,1)}) %all-reduce.25.cloned.1.call-update) | async-done | bytes 3145744 | tf_op jit(solution)/shard_map/psum | solution.py:396
  669.3 20.4 %fusion.77 = f32[1,2048,3,64]{1,3,2,0:T(8,128)} fusion(f32[1,2048,3,64]{1,3,2,0:T(8,128)} %copy-done.9, f32[1,2048,3,64]{1,3,2,0:T(8,128)} %get-tuple-element.290, bf16[2048,3,64]{0,2,1:T(8,128)(2,1)} %copy-done.5, f32[3,2048,2048]{1,2,0:T(8,128)} %get-tuple-element.286, f32[3,2048]{1,0:T(4,128)S(1)} %log_add_fusion), kind=kOutput, calls=%fused_computation.119 | convolution fusion | flops 1674313728 | bytes 55861248 | tf_op jit(solution)/shard_map/bhnm,bmhc->bnhc/dot_general | solution.py:143
  696.8 19.3 %fusion.124 = f32[3,64,2048]{2,1,0:T(8,128)} fusion(bf16[2048,3,64]{0,2,1:T(8,128)(2,1)S(1)} %bitcast.291, f32[3,2048,2048]{1,2,0:T(8,128)} %fusion.1), kind=kOutput, calls=%fused_computation.184 | convolution fusion | flops 1623195648 | bytes 52690944 | tf_op jit(solution)/shard_map/while/body/eval_jaxpr/bhnm,bnhc->bmhc/dot_general | solution.py:192
  716.0 19.3 %fusion.71 = bf16[3,64,2048]{2,1,0:T(8,128)(2,1)S(1)} fusion(bf16[2048,3,64]{0,2,1:T(8,128)(2,1)S(1)} %bitcast.292, f32[3,2048,2048]{1,2,0:T(8,128)} %get-tuple-element.286, f32[3,2048]{1,0:T(4,128)S(1)} %log_add_fusion), kind=kOutput, calls=%fused_computation.116 | convolution fusion | flops 1636171776 | bytes 51929088 | tf_op jit(solution)/shard_map/bhnm,bnhc->bmhc/dot_general | solution.py:192
  735.4 31.9 %fusion.84 = f32[3,2048]{1,0:T(4,128)S(1)} fusion(bf16[3,2048,64]{1,2,0:T(8,128)(2,1)S(1)} %bitcast.293, f32[1,2048,3,64]{1,3,2,0:T(8,128)S(1)} %copy-done.12, bf16[2048,3,64]{0,2,1:T(8,128)(2,1)S(1)} %bitcast.297, f32[3,2048,2048]{1,2,0:T(8,128)} %fusion.1), kind=kOutput, calls=%fused_computation.132 | convolution fusion | flops 1662511104 | bytes 53501952 | tf_op jit(solution)/shard_map/while/body/eval_jaxpr/bhnm,bmhc->bnhc/dot_general | solution.py:143
  767.2 25.9 %multiply_convert_fusion = bf16[3,2048,2048]{1,2,0:T(8,128)(2,1)} fusion(f32[3,2048,2048]{1,2,0:T(8,128)} %fusion.1, f32[3,2048]{1,0:T(4,128)S(1)} %fusion.84, bf16[2048,3,64]{0,2,1:T(8,128)(2,1)S(1)} %bitcast.294, bf16[2048,3,64]{0,2,1:T(8,128)(2,1)S(1)} %bitcast.298), kind=kOutput, calls=%fused_computation.9 | convolution fusion | flops 1648361472 | bytes 77094912 | tf_op jit(solution)/shard_map/while/body/eval_jaxpr/bnhc,bmhc->bhnm/dot_general | solution.py:172
  793.2 25.8 %multiply_convert_fusion.1 = bf16[3,2048,2048]{1,2,0:T(8,128)(2,1)} fusion(f32[3,2048,2048]{1,2,0:T(8,128)} %get-tuple-element.286, f32[3,2048]{1,0:T(4,128)S(1)} %fusion.84, f32[3,2048]{1,0:T(4,128)S(1)} %log_add_fusion, bf16[2048,3,64]{0,2,1:T(8,128)(2,1)S(1)} %bitcast.295, bf16[2048,3,64]{0,2,1:T(8,128)(2,1)S(1)} %copy-done.6), kind=kOutput, calls=%fused_computation.10 | convolution fusion | flops 1660944384 | bytes 77119488 | tf_op jit(solution)/shard_map/bnhc,bmhc->bhnm/dot_general | solution.py:172
  819.0 13.9 %convolution_multiply_fusion = f32[3,64,2048]{2,1,0:T(8,128)} fusion(bf16[2048,3,64]{0,2,1:T(8,128)(2,1)S(1)} %copy-done.8, bf16[3,2048,2048]{1,2,0:T(8,128)(2,1)} %multiply_convert_fusion), kind=kOutput, calls=%fused_computation.107 | convolution fusion | flops 1611005952 | bytes 27525120 | tf_op jit(solution)/shard_map/while/body/eval_jaxpr/bhnm,bnhc->bmhc/dot_general | solution.py:189
  832.9 12.5 fusion.70
  848.2 12.2 convert_reduce_fusion.3
  860.3 12.2 convert_reduce_fusion.1
  926.0 13.2 %fusion.144 = (bf16[3,64]{1,0:T(4,128)(2,1)S(1)}, bf16[1,2048,3,64]{1,3,2,0:T(8,128)(2,1)S(1)}) fusion(f32[1,2048,3,64]{1,3,2,0:T(8,128)S(1)} %copy-done.26, f32[3,64,2048]{2,1,0:T(8,128)S(1)} %fusion.146, bf16[2048,3,64]{0,2,1:T(8,128)(2,1)S(1)} %bitcast.302, bf16[3,2048,2048]{1,2,0:T(8,128)(2,1)} %multiply_convert_fusion), kind=kOutput, calls=%fused_computation.196 | convolution fusion | flops 1612578560 | bytes 29884800 | tf_op jit(solution)/shard_map/while/body/eval_jaxpr/bhnm,bmhc->bnhc/dot_general | solution.py:178
  939.2 21.8 %collective-permute-done.3 = bf16[1,2048,384]{1,2,0:T(8,128)(2,1)S(1)} collective-permute-done((bf16[1,2048,384]{1,2,0:T(8,128)(2,1)S(1)}, bf16[1,2048,384]{1,2,0:T(8,128)(2,1)S(1)}, u32[]{:S(2)}, u32[]{:S(2)}) %collective-permute-start.3) | collective-permute-done | bytes 1572896 | tf_op jit(solution)/shard_map/ppermute | solution.py:18
  1013.5 21.5 %reduce-scatter.21.cloned.1.call-done = bf16[127,16]{0,1:T(8,128)(2,1)} async-done(((bf16[127,64]{0,1:T(8,128)(2,1)}), bf16[127,16]{0,1:T(8,128)(2,1)}) %reduce-scatter.21.cloned.1.call-update) | async-done | bytes 4080 | tf_op jit(solution)/shard_map/reduce_scatter | solution.py:512
  1035.0 21.7 %reduce-scatter.23.cloned.1.call-done = bf16[127,16]{0,1:T(8,128)(2,1)} async-done(((bf16[127,64]{0,1:T(8,128)(2,1)}), bf16[127,16]{0,1:T(8,128)(2,1)}) %reduce-scatter.23.cloned.1.call-update) | async-done | bytes 4080 | tf_op jit(solution)/shard_map/reduce_scatter | solution.py:515
  1056.7 14.2 %all-reduce.12 = (bf16[127,16]{0,1:T(8,128)(2,1)S(1)}, bf16[127,16]{0,1:T(8,128)(2,1)S(1)}) all-reduce(bf16[127,16]{0,1:T(8,128)(2,1)} %reduce-scatter.21.cloned.1.call-done, bf16[127,16]{0,1:T(8,128)(2,1)} %reduce-scatter.23.cloned.1.call-done), channel_id=1, replica_groups=mesh['dp'=4,'ctx'=2,'tensor'=4] {'tensor'}, use_global_device_ids=true, to_apply=%region_32.33 | all-reduce | flops 4064 | bytes 16256 | tf_op jit(solution)/shard_map/psum | solution.py:490
  1087.1 170.0 %all-reduce.27.cloned.1.call-done = (bf16[1,2048,768]{2,1,0:T(8,128)(2,1)}, bf16[1,2048,768]{2,1,0:T(8,128)(2,1)}) async-done(((bf16[1,2048,768]{2,1,0:T(8,128)(2,1)}, bf16[1,2048,768]{2,1,0:T(8,128)(2,1)}), (bf16[1,2048,768]{2,1,0:T(8,128)(2,1)}, bf16[1,2048,768]{2,1,0:T(8,128)(2,1)})) %all-reduce.27.cloned.1.call-update) | async-done | bytes 6291472 | tf_op jit(solution)/shard_map/psum | solution.py:52
  1266.6 11.2 all-reduce.14
  1292.4 12.8 add_add_fusion.2
  (368 shorter events, 291.0 us)
Async XLA Ops:
  8.0 44.0 %copy-start = (bf16[1,2048,768]{2,1,0:T(8,128)(2,1)S(1)}, bf16[1,2048,768]{2,1,0:T(8,128)(2,1)}, u32[]{:S(2)}) copy-start(bf16[1,2048,768]{2,1,0:T(8,128)(2,1)} %param.16) | copy-start | bytes 9437188
  8.0 472.3 %all-reduce.23.cloned.1.call-start = ((), (), s32[]{:S(2)}) async-start(), calls=%async_computation.8 | async-start | bytes 6291456 | tf_op jit(solution)/shard_map/psum | solution.py:52
  58.4 226.4 %collective-permute-start.1 = (bf16[1,2048,384]{1,2,0:T(8,128)(2,1)}, bf16[1,2048,384]{1,2,0:T(8,128)(2,1)}, u32[]{:S(2)}, u32[]{:S(2)}) collective-permute-start(bf16[1,2048,384]{1,2,0:T(8,128)(2,1)} %pad_maximum_fusion), channel_id=1, source_target_pairs={{0,4},{4,0},{1,5},{5,1},{2,6},{6,2},{3,7},{7,3},{8,12},{12,8},{9,1... | collective-permute-start | bytes 4718600 | tf_op jit(solution)/shard_map/while/body/eval_jaxpr/ppermute | solution.py:18
  60.0 84.7 %copy-start.15 = (bf16[1,2048,1,192]{1,3,2,0:T(8,128)(2,1)}, bf16[1,2048,1,192]{1,3,2,0:T(8,128)(2,1)S(1)}, u32[]{:S(2)}) copy-start(bf16[1,2048,1,192]{1,3,2,0:T(8,128)(2,1)S(1)} %slice.74) | copy-start | bytes 2359300
  63.1 121.9 %collective-permute-start = (bf16[1,393216]{1,0:T(2,128)(2,1)}, bf16[1,393216]{1,0:T(2,128)(2,1)}, u32[]{:S(2)}, u32[]{:S(2)}) collective-permute-start(bf16[1,393216]{1,0:T(2,128)(2,1)} %convert_element_type.401), channel_id=1, source_target_pairs={{0,4},{4,0},{1,5},{5,1},{2,6},{6,2},{3,7},{7,3},{8,12},{12,8},{9,1... | collective-permute-start | bytes 2359304 | tf_op jit(solution)/shard_map/while/body/eval_jaxpr/ppermute | solution.py:18
  110.0 176.3 %copy-start.7 = (bf16[2048,3,64]{0,2,1:T(8,128)(2,1)}, bf16[2048,3,64]{0,2,1:T(8,128)(2,1)S(1)}, u32[]{:S(2)}) copy-start(bf16[2048,3,64]{0,2,1:T(8,128)(2,1)S(1)} %add_convert_fusion.5) | copy-start | bytes 2359300
  144.8 40.0 %copy-start.37 = (f32[1,2048,1,192]{1,3,2,0:T(8,128)S(1)}, f32[1,2048,1,192]{1,3,2,0:T(8,128)}, u32[]{:S(2)}) copy-start(f32[1,2048,1,192]{1,3,2,0:T(8,128)} %get-tuple-element.269) | copy-start | bytes 4718596
  185.0 150.8 %copy-start.5 = (bf16[2048,3,64]{0,2,1:T(8,128)(2,1)}, bf16[2048,3,64]{0,2,1:T(8,128)(2,1)S(1)}, u32[]{:S(2)}) copy-start(bf16[2048,3,64]{0,2,1:T(8,128)(2,1)S(1)} %add_convert_fusion.6) | copy-start | bytes 2359300
  355.4 124.9 %copy-start.1 = (bf16[1,2048,768]{2,1,0:T(8,128)(2,1)S(1)}, bf16[1,2048,768]{2,1,0:T(8,128)(2,1)}, u32[]{:S(2)}) copy-start(bf16[1,2048,768]{2,1,0:T(8,128)(2,1)} %param.16) | copy-start | bytes 9437188
  359.0 126.3 %all-gather.3.cloned.1.call-start = ((), (), s32[]{:S(2)}) async-start(), calls=%async_computation.9 | async-start | bytes 1474560 | tf_op jit(solution)/shard_map/all_gather | solution.py:44
  359.6 145.8 %all-gather.5.cloned.1.call-start = ((), (), s32[]{:S(2)}) async-start(), calls=%async_computation.10 | async-start | bytes 1474560 | tf_op jit(solution)/shard_map/all_gather | solution.py:46
  360.2 282.2 %all-reduce.25.cloned.1.call-start = ((), (), s32[]{:S(2)}) async-start(), calls=%async_computation.11 | async-start | bytes 6291456 | tf_op jit(solution)/shard_map/psum | solution.py:396
  365.7 296.1 %copy-start.62 = (f32[768]{0:T(1024)}, f32[768]{0:T(1024)S(1)}, u32[]{:S(2)}) copy-start(f32[768]{0:T(1024)S(1)} %convert_element_type.412) | copy-start | bytes 9220
  365.7 296.1 %copy-start.54 = (f32[768]{0:T(1024)}, f32[768]{0:T(1024)S(1)}, u32[]{:S(2)}) copy-start(f32[768]{0:T(1024)S(1)} %convert_element_type.411) | copy-start | bytes 9220
  483.4 178.4 %copy-start.50 = (f32[2048]{0:T(1024)}, f32[2048]{0:T(1024)S(1)}, u32[]{:S(2)}) copy-start(f32[2048]{0:T(1024)S(1)} %broadcast_multiply_fusion) | copy-start | bytes 24580
  485.2 176.6 %copy-start.60 = (f32[2048]{0:T(1024)}, f32[2048]{0:T(1024)S(1)}, u32[]{:S(2)}) copy-start(f32[2048]{0:T(1024)S(1)} %fusion.121) | copy-start | bytes 24580
  522.2 465.6 %reduce-scatter.27.cloned.1.call-start = ((), (), s32[]{:S(2)}) async-start(), calls=%async_computation.18 | async-start | bytes 491520
  661.7 327.7 %reduce-scatter.17.cloned.1.call-start = ((), (), s32[]{:S(2)}) async-start(), calls=%async_computation.13 | async-start | bytes 1474560 | tf_op jit(solution)/shard_map/reduce_scatter | solution.py:530
  669.2 320.1 %reduce-scatter.19.cloned.1.call-start = ((), (), s32[]{:S(2)}) async-start(), calls=%async_computation.14 | async-start | bytes 1474560 | tf_op jit(solution)/shard_map/reduce_scatter | solution.py:536
  693.6 297.5 %reduce-scatter.15.cloned.1.call-start = ((), (), s32[]{:S(2)}) async-start(), calls=%async_computation.12 | async-start | bytes 1474560 | tf_op jit(solution)/shard_map/reduce_scatter | solution.py:506
  846.7 76.5 %collective-permute-start.2 = (bf16[1,2048,384]{1,2,0:T(8,128)(2,1)}, bf16[1,2048,384]{1,2,0:T(8,128)(2,1)}, u32[]{:S(2)}, u32[]{:S(2)}) collective-permute-start(bf16[1,2048,384]{1,2,0:T(8,128)(2,1)} %pad_maximum_fusion.1), channel_id=1, source_target_pairs={{0,4},{4,0},{1,5},{5,1},{2,6},{6,2},{3,7},{7,3},{8,12},{12,8},{9,1... | collective-permute-start | bytes 4718600 | tf_op jit(solution)/shard_map/while/body/eval_jaxpr/ppermute | solution.py:18
  925.3 37.1 %copy-start.2 = (bf16[1,2048,768]{2,1,0:T(8,128)(2,1)S(1)}, bf16[1,2048,768]{2,1,0:T(8,128)(2,1)}, u32[]{:S(2)}) copy-start(bf16[1,2048,768]{2,1,0:T(8,128)(2,1)} %param.16) | copy-start | bytes 9437188
  925.3 37.1 %copy-start.53 = (f32[2048]{0:T(1024)S(1)}, f32[2048]{0:T(1024)}, u32[]{:S(2)}) copy-start(f32[2048]{0:T(1024)} %copy-done.52) | copy-start | bytes 24580
  925.4 37.1 %copy-start.66 = (f32[2048]{0:T(1024)S(1)}, f32[2048]{0:T(1024)}, u32[]{:S(2)}) copy-start(f32[2048]{0:T(1024)} %copy-done.65) | copy-start | bytes 24580
  925.4 35.7 %collective-permute-start.3 = (bf16[1,2048,384]{1,2,0:T(8,128)(2,1)S(1)}, bf16[1,2048,384]{1,2,0:T(8,128)(2,1)S(1)}, u32[]{:S(2)}, u32[]{:S(2)}) collective-permute-start(bf16[1,2048,384]{1,2,0:T(8,128)(2,1)S(1)} %fusion.37), channel_id=1, source_target_pairs={{0,4},{4,0},{1,5},{5,1},{2,6},{6,2},{3,7},{7,3},{8,12},{12,8},{9,1... | collective-permute-start | bytes 4718600 | tf_op jit(solution)/shard_map/ppermute | solution.py:18
  966.9 45.9 %reduce-scatter.29.cloned.1.call-start = ((), (), s32[]{:S(2)}) async-start(), calls=%async_computation.19 | async-start | bytes 20480
  967.8 67.2 %reduce-scatter.21.cloned.1.call-start = ((), (), s32[]{:S(2)}) async-start(), calls=%async_computation.15 | async-start | bytes 20480 | tf_op jit(solution)/shard_map/reduce_scatter | solution.py:512
  981.3 75.4 %reduce-scatter.23.cloned.1.call-start = ((), (), s32[]{:S(2)}) async-start(), calls=%async_computation.16 | async-start | bytes 20480 | tf_op jit(solution)/shard_map/reduce_scatter | solution.py:515
  986.7 92.5 %reduce-scatter.25.cloned.1.call-start = ((), (), s32[]{:S(2)}) async-start(), calls=%async_computation.17 | async-start | bytes 20480
  987.7 92.4 %all-reduce.29.cloned.1.call-start = ((), (), s32[]{:S(2)}) async-start(), calls=%async_computation.21 | async-start | bytes 1966080 | tf_op jit(solution)/shard_map/psum | solution.py:546
  991.1 265.9 %all-reduce.27.cloned.1.call-start = ((), (), s32[]{:S(2)}) async-start(), calls=%async_computation.20 | async-start | bytes 12582912 | tf_op jit(solution)/shard_map/psum | solution.py:52
  1002.2 258.1 %copy-start.70 = (f32[2048]{0:T(1024)S(1)}, f32[2048]{0:T(1024)}, u32[]{:S(2)}) copy-start(f32[2048]{0:T(1024)} %copy-done.69) | copy-start | bytes 24580
  (76 other events, 922.4 us)
Sparse Core Ops, SparseCore 0:
  359.1 121.1 all-reduce.22
  522.3 120.0 all-reduce.24
  991.7 38.7 all-reduce.28
  1033.3 223.7 all-reduce.26
Sparse Core Ops, SparseCore 1:
  361.0 17.3 all-gather.2
  379.8 17.3 all-gather.4
  661.8 19.8 reduce-scatter.26
  684.2 25.6 reduce-scatter.16
  712.6 25.6 reduce-scatter.18
  967.0 24.1 reduce-scatter.14
  993.4 19.3 reduce-scatter.28
  1015.7 19.2 reduce-scatter.20
  1037.3 19.3 reduce-scatter.22
  1059.8 19.3 reduce-scatter.24
where the time goes:
time: 1320 us; the launch traced here: 1310 us
  waiting for transfers between devices  490 us (37%)
  matrix products  434 us (33%)
  other arithmetic  188 us (14%)
  blocking collectives  88.8 us (7%)
  local copies, waits for them, and re-layouts  88.7 us (7%)
  between operations  18.4 us (1%)
    psum x2, waiting for transfers between devices, head_total(): return lax.psum(pieces.astype(jnp.bfloat16), 'tensor').astype(jnp.float32)  285 us
    psum x1, waiting for transfers between devices, per_device(): lax.psum(jnp.einsum('bnf,df->bnd', grad_hidden, weight_in, preferred_elem...  120 us
    dot_general x3, matrix products, score_block(): jnp.einsum('bnhc,bmhc->bhnm', query4, key4, preferred_element_type=jnp.fl...  97.5 us
    dot_general x2, matrix products, contribute(): jnp.einsum('bhnm,bmhc->bnhc', rest, value4, preferred_element_type=jnp.fl...  52.2 us
    dot_general x2, matrix products, contribute(): jnp.einsum('bnhc,bmhc->bhnm', grad_heads4, value4, preferred_element_type...  51.7 us
    reduce_sum x1, other arithmetic, update(): jnp.sum(jnp.exp(scores - new_top[..., None]), axis=-1)  46.8 us
    dot_general x2, matrix products, contribute(): jnp.einsum('bhnm,bnhc->bmhc', weights.astype(jnp.bfloat16), grad_heads4,...  38.5 us
    dot_general x2, matrix products, contribute(): jnp.einsum('bhnm,bmhc->bnhc', rounded, value4, preferred_element_type=jnp...  36.9 us
  transfers between devices with their start and end apart: 18, of which 9 were waited for; matrix products, arithmetic and copies ran while one was open for 42% of the time, Pallas kernels for 0%

commit v1 on v0

v1 whole, which is shorter than its diff:
```python
import functools

import jax
import jax.numpy as jnp
from jax import lax
from jax.experimental import pallas as pl
from jax.experimental.pallas import tpu as pltpu
from jax.sharding import PartitionSpec as P

HD = 64
GW = 64
EPS = 1e-06
f32 = jnp.float32
bf16 = jnp.bfloat16
VMEM = 56 * 2**20


def iota(shape, dim):
    return lax.broadcasted_iota(jnp.int32, shape, dim)


def dot(a, b, ca, cb):
    return lax.dot_general(a, b, (((ca,), (cb,)), ((), ())), preferred_element_type=f32)


def make_qaug(qT, tab, il0, off, R):
    bq = qT.shape[1]
    qf = jnp.concatenate([qT.astype(f32), jnp.zeros((64, bq), f32)], 0).T
    g = dot(qT, tab, 0, 0)
    lane = iota((64, 128), 1)
    used = (lane < 64 + R) | ((lane >= 96) & (lane < 96 + R))
    outs = []
    for k in range(bq // 64):
        gh = g[k * 64 : (k + 1) * 64, :128]
        gw = g[k * 64 : (k + 1) * 64, 128:]
        sh = 63 - (il0 + k) + off
        h64 = pltpu.roll(gh, lax.rem(64 - sh + 256, 128), 1)
        h96 = pltpu.roll(gh, lax.rem(96 - sh + 256, 128), 1)
        w64 = pltpu.roll(gw, 1, 1, stride=1, stride_axis=0)
        w0 = pltpu.roll(gw, 65, 1, stride=1, stride_axis=0)
        a = jnp.where(lane < 64, qf[k * 64 : (k + 1) * 64], w64)
        wl = w0 - w0.astype(bf16).astype(f32)
        hl = h96 - h96.astype(bf16).astype(f32)
        b = jnp.where(lane < 64, wl, jnp.where(lane < 96, h64, hl))
        b = jnp.where(used, b, 0.0)
        outs.append(jnp.concatenate([a, b], 1).astype(bf16))
    return jnp.concatenate(outs, 0)


def build_kaug(kT, kaug, flipped=False):
    KB = kT.shape[1]
    ck = min(512, KB)
    for c in range(KB // ck):
        kf = kT[:, c * ck : (c + 1) * ck].astype(f32) * 0.125
        kf = jnp.concatenate([kf, jnp.zeros((64, ck), f32)], 0).T
        n = iota((ck, 128), 0) + c * ck
        lane = iota((ck, 128), 1)
        col, row = n & 63, n >> 6
        spot = 127 - col if flipped else 64 + col
        a = jnp.where(lane < 64, kf, (lane == spot).astype(f32))
        b = jnp.where(lane < 64, (lane == col).astype(f32), ((lane & 31) == row).astype(f32))
        kaug[c * ck : (c + 1) * ck, :] = jnp.concatenate([a, b], 1).astype(bf16)


def build_kaugT(kT, kaugT):
    KB = kT.shape[1]
    ck = min(512, KB)
    for c in range(KB // ck):
        f = iota((64, ck), 0)
        n = iota((64, ck), 1) + c * ck
        col, row = n & 63, n >> 6
        sl = slice(c * ck, (c + 1) * ck)
        kaugT[0:64, sl] = (kT[:, sl].astype(f32) * 0.125).astype(bf16)
        oc = (f == col).astype(f32).astype(bf16)
        kaugT[64:128, sl] = oc
        kaugT[128:192, sl] = oc
        kaugT[192:256, sl] = ((f & 31) == row).astype(f32).astype(bf16)


def fwd_kernel(off_ref, qT_ref, kvT_ref, tab_ref, *rest, R, bk, first, last):
    if first:
        rest = (None, None) + rest
    oi_ref, mli_ref, o_ref, ml_ref, *rest = rest
    ob_ref = rest[0] if last else None
    kaug, vaug = rest[-2:]
    KB = kvT_ref.shape[1]
    bq = qT_ref.shape[1]
    qi = pl.program_id(1)

    @pl.when(qi == 0)
    def _():
        build_kaug(kvT_ref[0:64, :], kaug)
        vaug[0:64, :] = kvT_ref[64:128, :]
        vaug[64:80, :] = (iota((16, KB), 0) == 0).astype(f32).astype(bf16)

    qaug = make_qaug(qT_ref[...], tab_ref[:, :256], qi * (bq // 64), off_ref[0], R)
    if first:
        m = jnp.full((1, bq), -3e38, f32)
        o = jnp.zeros((80, bq), f32)
    else:
        m = mli_ref[0:1, :]
        o = jnp.concatenate([oi_ref[...], jnp.broadcast_to(mli_ref[1:2, :], (16, bq))], 0)
    for c in range(KB // bk):
        s = dot(kaug[c * bk : (c + 1) * bk, :], qaug, 1, 1)
        mn = jnp.maximum(m, jnp.max(s, axis=0, keepdims=True))
        al = jnp.exp(m - mn)
        p = jnp.exp(s - mn).astype(bf16)
        o = o * al + jnp.dot(vaug[:, c * bk : (c + 1) * bk], p, preferred_element_type=f32)
        m = mn
    l = o[64:65, :]
    o = o[:64]
    if last:
        o = o * (1.0 / l)
        m = m + jnp.log(l)
        ob_ref[...] = o.astype(bf16)
    o_ref[...] = o
    ml_ref[...] = jnp.concatenate([m, l, jnp.zeros((6, bq), f32)], 0)


def attn_fwd(off, qT, kvT, tab, state, last, R, bq=1024, bk=512):
    H, _, T = qT.shape
    KB = kvT.shape[2]
    bq, bk = min(bq, T), min(bk, KB)
    first = state is None
    qs = lambda r: pl.BlockSpec((None, r, bq), lambda h, i, o: (h, 0, i))
    ins = [
        qs(64),
        pl.BlockSpec((None, 128, KB), lambda h, i, o: (h, 0, 0)),
        pl.BlockSpec((64, 384), lambda h, i, o: (0, 0)),
    ] + ([] if first else [qs(64), qs(8)])
    outs = [qs(64), qs(8)] + ([qs(64)] if last else [])
    shapes = [jax.ShapeDtypeStruct((H, 64, T), f32), jax.ShapeDtypeStruct((H, 8, T), f32)]
    shapes += [jax.ShapeDtypeStruct((H, 64, T), bf16)] if last else []
    return pl.pallas_call(
        functools.partial(fwd_kernel, R=R, bk=bk, first=first, last=last),
        grid_spec=pltpu.PrefetchScalarGridSpec(
            num_scalar_prefetch=1,
            grid=(H, T // bq),
            in_specs=ins,
            out_specs=outs,
            scratch_shapes=[pltpu.VMEM((KB, 256), bf16), pltpu.VMEM((80, KB), bf16)],
        ),
        out_shape=shapes,
        compiler_params=pltpu.CompilerParams(vmem_limit_bytes=VMEM),
        cost_estimate=pl.CostEstimate(
            flops=2 * H * T * KB * 512, bytes_accessed=H * T * 1200, transcendentals=H * T * KB
        ),
        name="attn_fwd",
    )(off, qT, kvT, tab, *([] if first else state))


def bwd_kernel(off_ref, qT_ref, kvT_ref, tab_ref, doT_ref, o_ref, ml_ref, *rest, R, bk, first):
    if first:
        rest = (None, None) + rest
    dqi_ref, dti_ref, dq_ref, dt_ref, dkv_ref, kaug, kaugT, vaug, acc = rest
    KB = kvT_ref.shape[1]
    bq = qT_ref.shape[1]
    hi, qi = pl.program_id(0), pl.program_id(1)

    @pl.when(qi == 0)
    def _():
        build_kaug(kvT_ref[0:64, :], kaug, True)
        build_kaugT(kvT_ref[0:64, :], kaugT)
        vaug[0:64, :] = kvT_ref[64:128, :]
        vaug[64:128, :] = (iota((64, KB), 0) < 3).astype(f32).astype(bf16)
        acc[...] = jnp.zeros_like(acc)

    @pl.when((qi == 0) & (hi == 0))
    def _():
        dt_ref[...] = jnp.zeros_like(dt_ref) if first else dti_ref[...]

    qT = qT_ref[...]
    doT = doT_ref[...]
    il0 = qi * (bq // 64)
    qaug = make_qaug(qT, tab_ref[:, :256], il0, off_ref[0], R)
    dof = doT.astype(f32)
    nd = -jnp.sum(dof * o_ref[...], axis=0, keepdims=True)
    d1 = nd.astype(bf16).astype(f32)
    d2 = (nd - d1).astype(bf16).astype(f32)
    d3 = nd - d1 - d2
    rid = iota((64, bq), 0)
    ext = jnp.where(rid == 2, d3, jnp.where(rid == 3, ml_ref[0:1, :], 0.0))
    ext = jnp.where(rid == 0, d1, jnp.where(rid == 1, d2, ext))
    t = jnp.concatenate([dof, ext], 0).T
    lse = t[:, 67:68]
    doaug = t.astype(bf16)
    dq = jnp.zeros((bq, 256), f32)
    for c in range(KB // bk):
        sl = slice(c * bk, (c + 1) * bk)
        s = jnp.dot(qaug, kaugT[:, sl], preferred_element_type=f32)
        p = jnp.exp(s - lse)
        dp = jnp.dot(doaug, vaug[:, sl], preferred_element_type=f32)
        pb = p.astype(bf16)
        ds = (p * dp).astype(bf16)
        acc[64:128, sl] += jnp.dot(doT, pb, preferred_element_type=f32)
        acc[0:64, sl] += jnp.dot(qT, ds, preferred_element_type=f32)
        dq += jnp.dot(ds, kaug[sl, :], preferred_element_type=f32)
    lane = iota((64, 128), 1)
    his, los = [], []
    for k in range(bq // 64):
        a = dq[k * 64 : (k + 1) * 64, :128]
        b = dq[k * 64 : (k + 1) * 64, 128:]
        gw = pltpu.roll(jnp.where(lane >= 64, a, 0.0), 64, 1, stride=1, stride_axis=0)
        sh = off_ref[0] - (il0 + k) - 1
        gh = pltpu.roll(
            jnp.where((lane >= 64) & (lane < 64 + R), b, 0.0), lax.rem(sh + 256, 128), 1
        )
        g = jnp.concatenate([gh, gw], 1)
        h = g.astype(bf16)
        his.append(h)
        los.append((g - h.astype(f32)).astype(bf16))
    gh = jnp.concatenate(his, 0)
    gl = jnp.concatenate(los, 0)
    tab = jnp.concatenate([tab_ref[:, :128], tab_ref[:, 256:]], 1)
    dqT = dq[:, :128].T[:64] + dot(tab, gh, 1, 1) + dot(tab, gl, 1, 1)
    dq_ref[...] = dqT if first else dqT + dqi_ref[...]
    dt_ref[...] += dot(qT, gh, 1, 0) + dot(qT, gl, 1, 0)

    @pl.when(qi == pl.num_programs(1) - 1)
    def _():
        dkv_ref[0:64, :] = (acc[0:64, :] * 0.125).astype(dkv_ref.dtype)
        dkv_ref[64:128, :] = acc[64:128, :].astype(dkv_ref.dtype)


def attn_bwd(off, qT, kvT, tab, doT, o, ml, state, dt, R, bq=1024, bk=512):
    H, _, T = qT.shape
    KB = kvT.shape[2]
    bq, bk = min(bq, T), min(bk, KB)
    first = state is None
    qs = lambda r: pl.BlockSpec((None, r, bq), lambda h, i, o: (h, 0, i))
    kvs = pl.BlockSpec((None, 128, KB), lambda h, i, o: (h, 0, 0))
    ts = pl.BlockSpec((64, 256), lambda h, i, o: (0, 0))
    tabs = pl.BlockSpec((64, 384), lambda h, i, o: (0, 0))
    ins = [qs(64), kvs, tabs, qs(64), qs(64), qs(8)] + ([] if first else [qs(64), ts])
    return pl.pallas_call(
        functools.partial(bwd_kernel, R=R, bk=bk, first=first),
        grid_spec=pltpu.PrefetchScalarGridSpec(
            num_scalar_prefetch=1,
            grid=(H, T // bq),
            in_specs=ins,
            out_specs=[qs(64), ts, kvs],
            scratch_shapes=[
                pltpu.VMEM((KB, 256), bf16),
                pltpu.VMEM((256, KB), bf16),
                pltpu.VMEM((128, KB), bf16),
                pltpu.VMEM((128, KB), f32),
            ],
        ),
        out_shape=[
            jax.ShapeDtypeStruct((H, 64, T), f32),
            jax.ShapeDtypeStruct((64, 256), f32),
            jax.ShapeDtypeStruct((H, 128, KB), dt),
        ],
        compiler_params=pltpu.CompilerParams(vmem_limit_bytes=VMEM),
        cost_estimate=pl.CostEstimate(
            flops=2 * H * T * KB * 1024, bytes_accessed=H * T * 2000, transcendentals=H * T * KB
        ),
        name="attn_bwd",
    )(off, qT, kvT, tab, doT, o, ml, *([] if first else state))


def mlp1_kernel(h2_ref, g_ref, wi_ref, wo_ref, b_ref, a_ref, du_ref, dh_ref, db_ref):
    fb = wi_ref.shape[-1]
    wi = wi_ref[...].reshape(-1, fb)
    wo = wo_ref[...].reshape(-1, fb)
    u = jnp.dot(h2_ref[...], wi, preferred_element_type=f32) + b_ref[...].astype(f32)
    ga = jnp.dot(g_ref[...], wo, preferred_element_type=f32)
    cdf = 0.5 + 0.5 * lax.erf(u * 0.7071067811865476)
    a_ref[...] = (u * cdf).astype(bf16)
    slope = cdf + u * (jnp.exp(-0.5 * u * u) * 0.3989422804014327)
    du = (slope * ga).astype(bf16)
    du_ref[...] = du
    db_ref[...] = jnp.sum(du.astype(f32), axis=0, keepdims=True)
    dh = dot(du, wi, 1, 1)
    step = pl.program_id(0) * pl.num_programs(1) + pl.program_id(1)

    @pl.when(step == 0)
    def _():
        dh_ref[...] = dh

    @pl.when(step > 0)
    def _():
        dh_ref[...] += dh


def mlp1(h2, g, W, bias, ft):
    N, D = h2.shape
    nd, nt, dd, _ = W.shape
    fb = ft // 2
    full = pl.BlockSpec((N, D), lambda t, j: (0, 0))
    act = pl.BlockSpec((None, N, fb), lambda t, j: (t, 0, j))
    row = pl.BlockSpec((None, 1, fb), lambda t, j: (t, 0, j))
    return pl.pallas_call(
        mlp1_kernel,
        grid=(nt, 2),
        in_specs=[
            full,
            full,
            pl.BlockSpec((nd, None, dd, fb), lambda t, j: (0, t, 0, j)),
            pl.BlockSpec((nd, None, dd, fb), lambda t, j: (0, t, 0, 2 + j)),
            row,
        ],
        out_specs=[act, act, full, row],
        out_shape=[
            jax.ShapeDtypeStruct((nt, N, ft), bf16),
            jax.ShapeDtypeStruct((nt, N, ft), bf16),
            jax.ShapeDtypeStruct((N, D), f32),
            jax.ShapeDtypeStruct((nt, 1, ft), f32),
        ],
        compiler_params=pltpu.CompilerParams(vmem_limit_bytes=VMEM),
        cost_estimate=pl.CostEstimate(
            flops=6 * N * D * ft * nt, bytes_accessed=20 * 2**20, transcendentals=2 * N * ft * nt
        ),
        name="mlp_grad",
    )(h2, g, W, W, bias)


def mlp2_kernel(h2_ref, g_ref, da_ref, a_ref, du_ref, oT_ref, w_ref, y_ref, b_ref, gw_ref, out_ref, hT, gT, dT, acc):
    t = pl.program_id(0)
    ft = a_ref.shape[-1]

    @pl.when(t == 0)
    def _():
        hT[...] = h2_ref[...].T
        gT[...] = g_ref[...].T
        dT[...] = da_ref[...].T
        acc[...] = jnp.zeros_like(acc)

    nd, dd = gw_ref.shape[0], gw_ref.shape[1]
    a = a_ref[...]
    acc[...] += dot(a, w_ref[...].reshape(-1, ft), 1, 1)
    gw_ref[:, :, 0:ft] = (
        jnp.dot(hT[...], du_ref[...], preferred_element_type=f32).astype(bf16).reshape(nd, dd, ft)
    )
    gw_ref[:, :, ft : 2 * ft] = (
        jnp.dot(gT[...], a, preferred_element_type=f32).astype(bf16).reshape(nd, dd, ft)
    )
    gp = dot(dT[...], oT_ref[...], 1, 1).astype(bf16)
    gw_ref[:, :, 2 * ft :] = gp.reshape(nd, dd, gp.shape[-1])

    @pl.when(t == pl.num_programs(0) - 1)
    def _():
        out_ref[...] = (y_ref[...] + (acc[...] + b_ref[...].astype(f32))).astype(bf16)


def mlp2(h2, g, da, a, du, oT, W, y1, bias):
    N, D = h2.shape
    nd, nt, dd, cols = W.shape
    ft = a.shape[-1]
    kt = oT.shape[1]
    full = pl.BlockSpec((N, D), lambda t: (0, 0))
    act = pl.BlockSpec((None, N, ft), lambda t: (t, 0, 0))
    return pl.pallas_call(
        mlp2_kernel,
        grid=(nt,),
        in_specs=[
            full,
            full,
            full,
            act,
            act,
            pl.BlockSpec((None, kt, N), lambda t: (t, 0, 0)),
            pl.BlockSpec((nd, None, dd, ft), lambda t: (0, t, 0, 1)),
            full,
            pl.BlockSpec((1, D), lambda t: (0, 0)),
        ],
        out_specs=[pl.BlockSpec((nd, None, dd, cols), lambda t: (0, t, 0, 0)), full],
        out_shape=[
            jax.ShapeDtypeStruct((nd, nt, dd, cols), bf16),
            jax.ShapeDtypeStruct((N, D), bf16),
        ],
        scratch_shapes=[pltpu.VMEM((D, N), bf16)] * 3 + [pltpu.VMEM((N, D), f32)],
        compiler_params=pltpu.CompilerParams(vmem_limit_bytes=VMEM),
        cost_estimate=pl.CostEstimate(
            flops=7 * N * D * ft * nt, bytes_accessed=24 * 2**20, transcendentals=0
        ),
        name="mlp_weights",
    )(h2, g, da, a, du, oT, W, y1, bias)


def shift(value, axis, steps):
    n = lax.axis_size(axis)
    return lax.ppermute(value, axis, [(s, (s + steps) % n) for s in range(n)])


def flip(value, axis, bit):
    n = lax.axis_size(axis)
    return lax.ppermute(value, axis, [(s, s ^ bit) for s in range(n)])


def pick(value, index, dim=0):
    return lax.dynamic_index_in_dim(value, index, dim, keepdims=False)


def put(buffer, value, index):
    return lax.dynamic_update_index_in_dim(buffer, value, index, 0)


def gather_direct(value, axis):
    n = lax.axis_size(axis)
    me = lax.axis_index(axis)
    out = jnp.zeros((n,) + value.shape, value.dtype)
    out = put(out, value, me)
    for k in range(1, n):
        out = put(out, shift(value, axis, k), (me - k) % n)
    return out


def gather_dp(value):
    me = lax.axis_index("dp")
    far = flip(value, "dp", 2)
    out = jnp.zeros((4,) + value.shape, value.dtype)
    out = put(put(out, value, me), far, me ^ 2)
    out = put(out, flip(value, "dp", 1), me ^ 1)
    return put(out, flip(far, "dp", 1), me ^ 3)


def scatter_direct(value, axis):
    n = lax.axis_size(axis)
    me = lax.axis_index(axis)
    parts = [pick(value, me)]
    for k in range(1, n):
        parts.append(shift(pick(value, (me + k) % n), axis, k))
    return sum(p.astype(f32) for p in parts)


def exchange(value, axis):
    n = lax.axis_size(axis)
    me = lax.axis_index(axis)
    out = value
    for k in range(1, n):
        out = put(out, shift(pick(value, (me + k) % n), axis, k), (me - k) % n)
    return out


def scatter_dp(value):
    me = lax.axis_index("dp")
    core, x = me & 1, me >> 1
    v = value.reshape((2, 2) + value.shape[1:])
    pair = pick(v, core, 1).astype(f32) + flip(pick(v, 1 - core, 1), "dp", 1).astype(f32)
    pair = pair.astype(bf16)
    return pick(pair, x).astype(f32) + flip(pick(pair, 1 - x), "dp", 2).astype(f32)


def total_ctx(value):
    v = value.astype(bf16)
    if lax.axis_size("ctx") == 2:
        return v.astype(f32) + flip(v, "ctx", 1).astype(f32)
    return lax.psum(v.astype(f32), "ctx")


def norm_parts(x):
    c = x - jnp.mean(x, axis=-1, keepdims=True)
    r = lax.rsqrt(jnp.mean(c * c, axis=-1, keepdims=True) + EPS)
    return c * r, r


def norm_back(dh, gain, xhat, r):
    e = dh * gain
    return (
        e - jnp.mean(e, axis=-1, keepdims=True) - xhat * jnp.mean(e * xhat, axis=-1, keepdims=True)
    ) * r


def per_device(
    block_input,
    cotangent,
    norm1_gain,
    norm1_bias,
    qkv_weight,
    qkv_bias,
    rel_pos_h,
    rel_pos_w,
    proj_weight,
    proj_bias,
    norm2_gain,
    norm2_bias,
    mlp_in_weight,
    mlp_in_bias,
    mlp_out_weight,
    mlp_out_bias,
):
    nt, nc = lax.axis_size("tensor"), lax.axis_size("ctx")
    me, pos = lax.axis_index("tensor"), lax.axis_index("ctx")
    T = block_input.shape[1]
    D = block_input.shape[2]
    N = T // nt
    R = T // GW
    dd = D // 4
    H = qkv_bias.shape[1]
    E = H * HD
    x2 = block_input.reshape(T, D)
    g2 = cotangent.reshape(T, D)

    vec = jnp.concatenate(
        [
            v.reshape(-1)
            for v in (
                norm1_gain,
                norm1_bias,
                norm2_gain,
                norm2_bias,
                proj_bias,
                mlp_out_bias,
                qkv_bias,
                mlp_in_bias,
                rel_pos_h,
                rel_pos_w,
            )
        ]
    )
    vec = lax.all_gather(vec, "dp", axis=0)
    gain1, shift1, gain2, shift2, bproj, bout = (
        vec[:, i * dd : (i + 1) * dd].reshape(1, D).astype(f32) for i in range(6)
    )
    at = 6 * dd
    bq = vec[:, at : at + 2 * H * 16].reshape(4, 2, H, 16)
    bq = bq.transpose(1, 2, 0, 3).reshape(2, H, HD).astype(f32)
    at += 2 * H * 16
    nb = mlp_in_bias.size
    bin_t = vec[:, at : at + nb].reshape(4, nb // 16, 16).transpose(1, 0, 2).reshape(-1)
    at += nb
    L = rel_pos_h.shape[0]
    th = vec[:, at : at + L * 16].reshape(4, L, 16)
    tw = vec[:, at + L * 16 :].reshape(4, L, 16)
    zero = jnp.zeros((HD, 1), bf16)
    th = th.transpose(0, 2, 1).reshape(HD, L)
    tw = tw.transpose(0, 2, 1).reshape(HD, L)
    tab = jnp.concatenate([th[:, ::-1], zero, tw[:, ::-1], zero, tw, zero], 1)
    bin_all = lax.all_gather(bin_t, "tensor", axis=0)
    ft = bin_t.shape[0]

    wqkv = lax.all_gather(qkv_weight, "dp", axis=0, tiled=True)

    xf = x2.astype(f32)
    xh, _ = norm_parts(xf)
    h1 = (xh * gain1 + shift1).astype(bf16)
    wkv = wqkv[:, 1:].reshape(D, 2, H, HD).transpose(0, 2, 1, 3).reshape(D, H * 2 * HD)
    bkv = jnp.stack([jnp.zeros_like(bq[1]), bq[1]], 1).reshape(H * 2 * HD, 1)
    kvT = (dot(wkv, h1, 0, 1) + bkv).astype(bf16).reshape(H, 2 * HD, T)
    kv_far = [shift(kvT, "ctx", k) for k in range(1, nc)]
    qT = (dot(wqkv[:, 0], h1, 0, 1) + bq[0].reshape(E, 1)).astype(bf16).reshape(H, HD, T)

    pack = jnp.concatenate([mlp_in_weight, mlp_out_weight.T, proj_weight.T], 1)
    W = gather_dp(gather_direct(pack, "tensor"))
    wq_full = gather_dp(gather_direct(qkv_weight.reshape(dd, 3 * E), "tensor"))

    offs = [(((pos - k) % nc) - pos) * R for k in range(nc)]
    offs = [jnp.reshape(o, (1,)).astype(jnp.int32) for o in offs]
    state = attn_fwd(offs[0], qT, kvT, tab, None, nc == 1, R)
    for k in range(1, nc):
        state = attn_fwd(offs[k], qT, kv_far[k - 1], tab, state[:2], k == nc - 1, R)
    o32, lse, o16 = state

    oT = exchange(o16.reshape(E, nt, N).transpose(1, 0, 2), "tensor")
    wp = W[:, :, :, 2 * ft :].transpose(0, 2, 1, 3).reshape(D, nt * E)
    xm = pick(x2.reshape(nt, N, D), me).astype(f32)
    gm = pick(g2.reshape(nt, N, D), me)
    gmf = gm.astype(f32)
    y1 = xm + (dot(oT.reshape(nt * E, N), wp, 0, 1) + bproj)
    xhat2, r2 = norm_parts(y1)
    h2 = (xhat2 * gain2 + shift2).astype(bf16)
    a, du, dh2, dbin = mlp1(h2, gm, W, bin_all.reshape(nt, 1, ft), ft)
    dy1 = gmf + norm_back(dh2, gain2, xhat2, r2)
    da = dy1.astype(bf16)
    doT = dot(wp, da, 0, 1).astype(bf16).reshape(nt, E, N)
    doT = exchange(doT, "tensor").transpose(1, 0, 2).reshape(H, HD, T)
    GW2, out = mlp2(h2, gm, da, a, du, oT, W, y1, bout.astype(bf16))
    block_out = gather_direct(out, "tensor").reshape(1, T, D)

    dstate = None
    far = []
    for k in range(1, nc):
        dq, dtab, dkv = attn_bwd(offs[k], qT, kv_far[k - 1], tab, doT, o32, lse, dstate, bf16, R)
        dstate = (dq, dtab)
        far.append(shift(dkv, "ctx", -k))
    dq, dtab, dkv = attn_bwd(offs[0], qT, kvT, tab, doT, o32, lse, dstate, f32, R)
    for f in far:
        dkv = dkv + f.astype(f32)
    dqkv = jnp.concatenate([dq, dkv], 1).astype(bf16)
    dall = exchange(dqkv.reshape(H * 3 * HD, nt, N).transpose(1, 0, 2), "tensor")

    wq = wq_full.reshape(4, nt, dd, 3, H, HD).transpose(0, 2, 1, 4, 3, 5).reshape(D, nt * 3 * E)
    dh1 = dot(dall.reshape(nt * 3 * E, N), wq, 0, 1)
    xhat1, r1 = norm_parts(xm)
    gin = (dy1 + norm_back(dh1, gain1, xhat1, r1)).astype(bf16)
    grad_input = gather_direct(gin, "tensor").reshape(1, T, D).astype(f32)

    gmine = scatter_direct(scatter_dp(GW2).astype(bf16), "tensor")
    gmine = total_ctx(gmine)
    g_in = gmine[:, :ft]
    g_out = gmine[:, ft : 2 * ft].T
    g_proj = gmine[:, 2 * ft :].T
    gq = dot(h1, dqkv.reshape(H * 3 * HD, T), 0, 1).astype(bf16)
    gq = total_ctx(scatter_dp(gq.reshape(4, dd, H * 3 * HD)))
    g_qkv = gq.reshape(dd, H, 3, HD).transpose(0, 2, 1, 3).reshape(dd, 3, E)

    dqf = dqkv.astype(f32)
    bsum = jnp.sum(dqf, axis=2).reshape(H, 3, HD)
    gbq = jnp.stack([bsum[:, 0], bsum[:, 2]])
    gbq = lax.dynamic_update_index_in_dim(jnp.zeros((2, nt, H, HD), f32), gbq, me, 1)
    flat = jnp.concatenate(
        [
            v.reshape(-1)
            for v in (
                jnp.sum(dh2 * xhat2, 0),
                jnp.sum(dh2, 0),
                jnp.sum(da.astype(f32), 0),
                jnp.sum(gmf, 0),
                dbin,
                gbq,
                dtab,
                jnp.sum(dh1 * xhat1, 0),
                jnp.sum(dh1, 0),
            )
        ]
    )
    flat = lax.psum(flat, ("dp", "ctx", "tensor"))
    dp = lax.axis_index("dp")
    gb2, gs2, gbp, gbo = (pick(flat[i * D : (i + 1) * D].reshape(4, dd), dp) for i in range(4))
    at = 4 * D
    gbin = flat[at : at + nt * ft].reshape(nt, ft // HD, 4, 16)
    gbin = pick(pick(gbin, me), dp, 1)
    at += nt * ft
    gbq = pick(pick(flat[at : at + 2 * nt * E].reshape(2, nt, H, 4, 16), me, 1), dp, 2)
    at += 2 * nt * E
    gtab = pick(flat[at : at + HD * 256].reshape(4, 16, 2, 128), dp)[:, :, :L]
    at += HD * 256
    gg1, gs1 = (pick(flat[at + i * D : at + (i + 1) * D].reshape(4, dd), dp) for i in range(2))
    return (
        block_out,
        grad_input,
        gg1,
        gs1,
        g_qkv,
        gbq,
        gtab[:, 0, ::-1].T,
        gtab[:, 1].T,
        g_proj,
        gbp,
        gb2,
        gs2,
        g_in,
        gbin,
        g_out,
        gbo,
    )


def solution(mesh):
    placed = (
        P("dp", "ctx", None),
        P("dp", "ctx", None),
        P("dp"),
        P("dp"),
        P("dp", None, "tensor"),
        P(None, "tensor", "dp"),
        P(None, "dp"),
        P(None, "dp"),
        P("tensor", "dp"),
        P("dp"),
        P("dp"),
        P("dp"),
        P("dp", "tensor"),
        P("tensor", "dp"),
        P("tensor", "dp"),
        P("dp"),
    )
    return jax.shard_map(
        per_device,
        mesh=mesh,
        in_specs=placed,
        out_specs=(placed[0], placed[0]) + placed[2:],
        check_vma=False,
    )
```

time: 1320 us -> 936 us (0.71)
  the two profiles are of different devices: /device:TPU:0 before, /device:TPU:14 now
where the time goes in v1:
time: 936 us; the launch traced here: 926 us
  waiting for transfers between devices  392 us (42%)
  local copies, waits for them, and re-layouts  217 us (23%)
  Pallas kernels  173 us (18%)
  starting transfers between devices  39.7 us (4%)
  other arithmetic  37.2 us (4%)
  blocking collectives  33.6 us (4%)
  matrix products  18.8 us (2%)
  between operations  15.1 us (2%)
    ppermute x26, waiting for transfers between devices, shift(): return lax.ppermute(value, axis, [(s, (s + steps) % n) for s in range(n)])  171 us
    psum x1, waiting for transfers between devices, per_device(): flat = lax.psum(flat, ('dp', 'ctx', 'tensor'))  164 us
    pallas_call x2, Pallas kernels, attn_bwd(): pl.pallas_call(functools.partial(bwd_kernel, R=R, bk=bk, first=first), gr...  83.1 us
    dynamic_update_slice x32, local copies, waits for them, and re-layouts, put(): return lax.dynamic_update_index_in_dim(buffer, value, index, 0)  74.5 us
    pallas_call x2, Pallas kernels, attn_fwd(): pl.pallas_call(functools.partial(fwd_kernel, R=R, bk=bk, first=first, las...  56.9 us
    ppermute x12, waiting for transfers between devices, flip(): return lax.ppermute(value, axis, [(s, s ^ bit) for s in range(n)])  56.3 us
    ppermute x26, starting transfers between devices, shift(): return lax.ppermute(value, axis, [(s, (s + steps) % n) for s in range(n)])  33.9 us
    unnamed x92, local copies, waits for them, and re-layouts  30.2 us
  transfers between devices with their start and end apart: 39, of which 15 were waited for; matrix products, arithmetic and copies ran while one was open for 26% of the time, Pallas kernels for 15%

profile of v1, /device:TPU:14, one launch (start us, length us, event | category | flops | bytes accessed | tf_op | source)
XLA Modules:
  0.0 926.4 jit_solution(15455022375600272325)
XLA Ops:
  18.3 4.1 concatenate.15
  22.4 5.3 all-gather.1
  36.3 13.4 %all_gather.14 = bf16[768,3,192]{2,1,0:T(4,128)(2,1)} all-gather(bf16[192,3,192]{2,1,0:T(4,128)(2,1)S(1)} %copy.144), channel_id=1, replica_groups=mesh['dp'=4,'ctx'=2,'tensor'=4] {'dp'}, dimensions={0}, use_global_device_ids=true | all-gather | bytes 1105920 | tf_op jit(solution)/shard_map/all_gather | solution.py:533
  75.5 4.0 fusion.10
  80.3 26.7 %attn_fwd.2 = (f32[3,64,2048]{2,1,0:T(8,128)}, f32[3,8,2048]{2,1,0:T(8,128)}) custom-call(s32[1]{0:T(128)} %bitcast.18.off_ref, bf16[3,64,2048]{2,1,0:T(8,128)(2,1)} %bitcast.319, bf16[3,128,2048]{2,1,0:T(8,128)(2,1)} %bitcast.13.kvT_ref, bf16[64,384]{1,0:T(8,128)(2,1)} %concatenate.16.tab_ref), custom_call_target="tpu_custom_call" | custom-call | flops 12884901888 | bytes 7372800 | tf_op jit(solution)/shard_map/attn_fwd/pallas_call | solution.py:134
  123.7 14.9 %all-gather.2.b_ref = bf16[4,1,768]{2,1,0:T(2,128)(2,1)} all-gather(bf16[1,1,768]{2,1,0:T(2,128)(2,1)S(1)} %reshape.471), channel_id=1, replica_groups=mesh['dp'=4,'ctx'=2,'tensor'=4] {'tensor'}, dimensions={0}, use_global_device_ids=true | all-gather | bytes 7680 | tf_op jit(solution)/shard_map/all_gather | solution.py:530
  153.8 5.1 broadcast_in_dim.142
  162.4 39.2 %collective-permute-done.23 = bf16[4,192,576]{2,1,0:T(8,128)(2,1)} collective-permute-done((bf16[4,192,576]{2,1,0:T(8,128)(2,1)}, bf16[4,192,576]{2,1,0:T(8,128)(2,1)}, u32[]{:S(2)}, u32[]{:S(2)}) %collective-permute-start.23) | collective-permute-done | bytes 884768 | tf_op jit(solution)/shard_map/ppermute | solution.py:388
  209.3 30.2 %attn_fwd.3 = (f32[3,64,2048]{2,1,0:T(8,128)}, f32[3,8,2048]{2,1,0:T(8,128)}, bf16[3,64,2048]{2,1,0:T(8,128)(2,1)}) custom-call(s32[1]{0:T(128)} %bitcast.2.off_ref, bf16[3,64,2048]{2,1,0:T(8,128)(2,1)} %bitcast.320, bf16[3,128,2048]{2,1,0:T(8,128)(2,1)} %collective-permute-done.kvT_ref, bf16[64,384]{1,0:T(8,128)(2,1)} %concatenate.16.tab_ref, ...), custom_call_target="tpu_custom_call" | custom-call | flops 12884901888 | bytes 7372800 | tf_op jit(solution)/shard_map/attn_fwd/pallas_call | solution.py:134
  251.8 8.8 collective-permute-done.1
  272.5 9.0 copy.171
  281.5 8.9 reshape.439
  304.9 4.0 reshape.429
  312.9 17.6 %mlp_grad.1 = (bf16[4,512,768]{2,1,0:T(8,128)(2,1)}, bf16[4,512,768]{2,1,0:T(8,128)(2,1)}, f32[512,768]{1,0:T(8,128)}, f32[4,1,768]{2,1,0:T(1,128)}) custom-call(bf16[512,768]{1,0:T(8,128)(2,1)} %add_convert_fusion.1.h2_ref, bf16[512,768]{1,0:T(8,128)(2,1)} %get-tuple-element.141.g_ref, ...), custom_call_target="tpu_custom_call" | custom-call | flops 7247757312 | bytes 20971520 | tf_op jit(solution)/shard_map/mlp_grad/pallas_call | solution.py:293
  337.1 15.4 %mlp_weights.1 = (bf16[4,4,192,1728]{3,2,1,0:T(8,128)(2,1)}, bf16[512,768]{1,0:T(8,128)(2,1)}) custom-call(bf16[512,768]{1,0:T(8,128)(2,1)} %add_convert_fusion.1.h2_ref, bf16[512,768]{1,0:T(8,128)(2,1)} %get-tuple-element.141.g_ref, bf16[512,768]{1,0:T(8,128)(2,1)} %copy-done.21, bf16[4,512,768]{2,1,0:T(8,128)(2,1)} %get-tuple-element.37.a_ref, ...), custom_call_target="tpu_custom_call" | custom-call | flops 8455716864 | bytes 25165824 | tf_op jit(solution)/shard_map/mlp_weights/pallas_call | solution.py:353
  359.5 5.4 dynamic-slice_bitcast_fusion
  374.6 58.3 %collective-permute-done.13 = bf16[192,512]{1,0:T(8,128)(2,1)S(1)} collective-permute-done((bf16[192,512]{1,0:T(8,128)(2,1)S(1)}, bf16[192,512]{1,0:T(8,128)(2,1)S(1)}, u32[]{:S(2)}, u32[]{:S(2)}) %collective-permute-start.13) | collective-permute-done | bytes 196640 | tf_op jit(solution)/shard_map/ppermute | solution.py:383
  437.1 8.1 dynamic_update_slice.125
  445.2 7.9 dynamic_update_slice.126
  453.1 7.9 dynamic_update_slice.127
  463.9 41.2 %attn_bwd.2 = (f32[3,64,2048]{2,1,0:T(8,128)}, f32[64,256]{1,0:T(8,128)}, bf16[3,128,2048]{2,1,0:T(8,128)(2,1)}) custom-call(s32[1]{0:T(128)} %bitcast.2.off_ref, bf16[3,64,2048]{2,1,0:T(8,128)(2,1)} %bitcast.321, bf16[3,128,2048]{2,1,0:T(8,128)(2,1)} %collective-permute-done.kvT_ref, bf16[64,384]{1,0:T(8,128)(2,1)} %concatenate.16.tab_ref, ...), custom_call_target="tpu_custom_call" | custom-call | flops 25769803776 | bytes 12288000 | tf_op jit(solution)/shard_map/attn_bwd/pallas_call | solution.py:235
  506.6 41.9 %attn_bwd.3 = (f32[3,64,2048]{2,1,0:T(8,128)}, f32[64,256]{1,0:T(8,128)}, f32[3,128,2048]{2,1,0:T(8,128)}) custom-call(s32[1]{0:T(128)} %bitcast.18.off_ref, bf16[3,64,2048]{2,1,0:T(8,128)(2,1)} %bitcast.322, bf16[3,128,2048]{2,1,0:T(8,128)(2,1)} %bitcast.13.kvT_ref, bf16[64,384]{1,0:T(8,128)(2,1)} %concatenate.16.tab_ref, ...), custom_call_target="tpu_custom_call" | custom-call | flops 25769803776 | bytes 12288000 | tf_op jit(solution)/shard_map/attn_bwd/pallas_call | solution.py:235
  559.0 5.5 convolution_convert_fusion
  568.8 6.2 convert_element_type.267
  587.7 5.8 collective-permute-done.17
  593.6 35.5 %collective-permute-done.18 = bf16[576,512]{1,0:T(8,128)(2,1)S(1)} collective-permute-done((bf16[576,512]{1,0:T(8,128)(2,1)S(1)}, bf16[576,512]{1,0:T(8,128)(2,1)S(1)}, u32[]{:S(2)}, u32[]{:S(2)}) %collective-permute-start.18) | collective-permute-done | bytes 589856 | tf_op jit(solution)/shard_map/ppermute | solution.py:383
  632.6 5.5 fusion
  655.9 164.2 %all-reduce.3.cloned.1.call-done = f32[25600]{0:T(1024)} async-done(((f32[25600]{0:T(1024)}), f32[25600]{0:T(1024)}) %all-reduce.3.cloned.1.call-update) | async-done | bytes 102416 | tf_op jit(solution)/shard_map/psum | solution.py:618
  830.7 3.7 collective-permute-done.31
  847.0 38.9 %collective-permute-done.34 = bf16[192,1728]{1,0:T(8,128)(2,1)S(1)} collective-permute-done((bf16[192,1728]{1,0:T(8,128)(2,1)S(1)}, bf16[192,1728]{1,0:T(8,128)(2,1)S(1)}, u32[]{:S(2)}, u32[]{:S(2)}) %collective-permute-start.34) | collective-permute-done | bytes 663584 | tf_op jit(solution)/shard_map/ppermute | solution.py:383
  885.9 10.4 %collective-permute-done.35 = bf16[192,1728]{1,0:T(8,128)(2,1)S(1)} collective-permute-done((bf16[192,1728]{1,0:T(8,128)(2,1)S(1)}, bf16[192,1728]{1,0:T(8,128)(2,1)S(1)}, u32[]{:S(2)}, u32[]{:S(2)}) %collective-permute-start.35) | collective-permute-done | bytes 663584 | tf_op jit(solution)/shard_map/ppermute | solution.py:383
  904.0 13.3 %collective-permute-done.37 = bf16[192,1728]{1,0:T(8,128)(2,1)S(1)} collective-permute-done((bf16[192,1728]{1,0:T(8,128)(2,1)S(1)}, bf16[192,1728]{1,0:T(8,128)(2,1)S(1)}, u32[]{:S(2)}, u32[]{:S(2)}) %collective-permute-start.37) | collective-permute-done | bytes 663584 | tf_op jit(solution)/shard_map/ppermute | solution.py:388
  (319 shorter events, 244.9 us)
Async XLA Ops:
  7.2 812.9 %all-reduce.3.cloned.1.call-start = ((), (), s32[]{:S(2)}) async-start(), calls=%async_computation | async-start | bytes 204800 | tf_op jit(solution)/shard_map/psum | solution.py:618
  10.3 99.3 %collective-permute-start.4 = (bf16[192,1728]{1,0:T(8,128)(2,1)}, bf16[192,1728]{1,0:T(8,128)(2,1)}, u32[]{:S(2)}, u32[]{:S(2)}) collective-permute-start(bf16[192,1728]{1,0:T(8,128)(2,1)} %pad_maximum_fusion), channel_id=1, source_target_pairs={{0,1},{1,2},{2,3},{3,0},{4,5},{5,6},{6,7},{7,4},{8,9},{9,10},{10,1... | collective-permute-start | bytes 1990664 | tf_op jit(solution)/shard_map/ppermute | solution.py:383
  11.9 103.2 %collective-permute-start.5 = (bf16[192,1728]{1,0:T(8,128)(2,1)}, bf16[192,1728]{1,0:T(8,128)(2,1)}, u32[]{:S(2)}, u32[]{:S(2)}) collective-permute-start(bf16[192,1728]{1,0:T(8,128)(2,1)} %pad_maximum_fusion), channel_id=1, source_target_pairs={{0,2},{1,3},{2,0},{3,1},{4,6},{5,7},{6,4},{7,5},{8,10},{9,11},{10,... | collective-permute-start | bytes 1990664 | tf_op jit(solution)/shard_map/ppermute | solution.py:383
  13.2 104.0 %collective-permute-start.6 = (bf16[192,1728]{1,0:T(8,128)(2,1)}, bf16[192,1728]{1,0:T(8,128)(2,1)}, u32[]{:S(2)}, u32[]{:S(2)}) collective-permute-start(bf16[192,1728]{1,0:T(8,128)(2,1)} %pad_maximum_fusion), channel_id=1, source_target_pairs={{0,3},{1,0},{2,1},{3,2},{4,7},{5,4},{6,5},{7,6},{8,11},{9,8},{10,9... | collective-permute-start | bytes 1990664 | tf_op jit(solution)/shard_map/ppermute | solution.py:383
  66.1 143.2 %collective-permute-start = (bf16[3,128,2048]{2,1,0:T(8,128)(2,1)}, bf16[3,128,2048]{2,1,0:T(8,128)(2,1)}, u32[]{:S(2)}, u32[]{:S(2)}) collective-permute-start(bf16[3,128,2048]{2,1,0:T(8,128)(2,1)} %bitcast.13.kvT_ref), channel_id=1, source_target_pairs={{0,4},{4,0},{1,5},{5,1},{2,6},{6,2},{3,7},{7,3},{8,12},{12,8},{9,1... | collective-permute-start | bytes 4718600 | tf_op jit(solution)/shard_map/ppermute | solution.py:383
  67.5 73.8 %collective-permute-start.20 = (bf16[192,576]{0,1:T(8,128)(2,1)}, bf16[192,576]{0,1:T(8,128)(2,1)}, u32[]{:S(2)}, u32[]{:S(2)}) collective-permute-start(bf16[192,576]{0,1:T(8,128)(2,1)} %bitcast.62), channel_id=1, source_target_pairs={{0,1},{1,2},{2,3},{3,0},{4,5},{5,6},{6,7},{7,4},{8,9},{9,10},{10,1... | collective-permute-start | bytes 663560 | tf_op jit(solution)/shard_map/ppermute | solution.py:383
  109.6 33.4 %collective-permute-start.21 = (bf16[192,576]{0,1:T(8,128)(2,1)}, bf16[192,576]{0,1:T(8,128)(2,1)S(1)}, u32[]{:S(2)}, u32[]{:S(2)}) collective-permute-start(bf16[192,576]{0,1:T(8,128)(2,1)} %bitcast.62), channel_id=1, source_target_pairs={{0,2},{1,3},{2,0},{3,1},{4,6},{5,7},{6,4},{7,5},{8,10},{9,11},{10,... | collective-permute-start | bytes 663560 | tf_op jit(solution)/shard_map/ppermute | solution.py:383
  115.1 28.6 %collective-permute-start.22 = (bf16[192,576]{0,1:T(8,128)(2,1)}, bf16[192,576]{0,1:T(8,128)(2,1)}, u32[]{:S(2)}, u32[]{:S(2)}) collective-permute-start(bf16[192,576]{0,1:T(8,128)(2,1)} %bitcast.62), channel_id=1, source_target_pairs={{0,3},{1,0},{2,1},{3,2},{4,7},{5,4},{6,5},{7,6},{8,11},{9,8},{10,9... | collective-permute-start | bytes 663560 | tf_op jit(solution)/shard_map/ppermute | solution.py:383
  119.2 89.6 %collective-permute-start.7 = (bf16[4,192,1728]{2,1,0:T(8,128)(2,1)}, bf16[4,192,1728]{2,1,0:T(8,128)(2,1)}, u32[]{:S(2)}, u32[]{:S(2)}) collective-permute-start(bf16[4,192,1728]{2,1,0:T(8,128)(2,1)} %bitcast_dynamic-update-slice_fusion.16), channel_id=1, source_target_pairs={{0,16},{8,24},{16,0},{24,8},{1,17},{9,25},{17,1},{25,9},{2,18},{10... | collective-permute-start | bytes 7962632 | tf_op jit(solution)/shard_map/ppermute | solution.py:388
  147.8 53.9 %collective-permute-start.23 = (bf16[4,192,576]{2,1,0:T(8,128)(2,1)}, bf16[4,192,576]{2,1,0:T(8,128)(2,1)}, u32[]{:S(2)}, u32[]{:S(2)}) collective-permute-start(bf16[4,192,576]{2,1,0:T(8,128)(2,1)} %copy.166), channel_id=1, source_target_pairs={{0,16},{8,24},{16,0},{24,8},{1,17},{9,25},{17,1},{25,9},{2,18},{10... | collective-permute-start | bytes 2654216 | tf_op jit(solution)/shard_map/ppermute | solution.py:388
  148.3 55.7 %collective-permute-start.24 = (bf16[4,192,576]{2,1,0:T(8,128)(2,1)}, bf16[4,192,576]{2,1,0:T(8,128)(2,1)}, u32[]{:S(2)}, u32[]{:S(2)}) collective-permute-start(bf16[4,192,576]{2,1,0:T(8,128)(2,1)} %copy.166), channel_id=1, source_target_pairs={{0,8},{8,0},{16,24},{24,16},{1,9},{9,1},{17,25},{25,17},{2,10},{10... | collective-permute-start | bytes 2654216 | tf_op jit(solution)/shard_map/ppermute | solution.py:388
  153.3 140.7 %collective-permute-start.8 = (bf16[4,192,1728]{2,1,0:T(8,128)(2,1)}, bf16[4,192,1728]{2,1,0:T(8,128)(2,1)}, u32[]{:S(2)}, u32[]{:S(2)}) collective-permute-start(bf16[4,192,1728]{2,1,0:T(8,128)(2,1)} %bitcast_dynamic-update-slice_fusion.16), channel_id=1, source_target_pairs={{0,8},{8,0},{16,24},{24,16},{1,9},{9,1},{17,25},{25,17},{2,10},{10... | collective-permute-start | bytes 7962632 | tf_op jit(solution)/shard_map/ppermute | solution.py:388
  204.0 63.8 %collective-permute-start.25 = (bf16[4,192,576]{2,1,0:T(8,128)(2,1)}, bf16[4,192,576]{2,1,0:T(8,128)(2,1)}, u32[]{:S(2)}, u32[]{:S(2)}) collective-permute-start(bf16[4,192,576]{2,1,0:T(8,128)(2,1)} %collective-permute-done.23), channel_id=1, source_target_pairs={{0,8},{8,0},{16,24},{24,16},{1,9},{9,1},{17,25},{25,17},{2,10},{10... | collective-permute-start | bytes 2654216 | tf_op jit(solution)/shard_map/ppermute | solution.py:388
  208.8 88.8 %collective-permute-start.9 = (bf16[4,192,1728]{2,1,0:T(8,128)(2,1)}, bf16[4,192,1728]{2,1,0:T(8,128)(2,1)}, u32[]{:S(2)}, u32[]{:S(2)}) collective-permute-start(bf16[4,192,1728]{2,1,0:T(8,128)(2,1)} %collective-permute-done.7), channel_id=1, source_target_pairs={{0,8},{8,0},{16,24},{24,16},{1,9},{9,1},{17,25},{25,17},{2,10},{10... | collective-permute-start | bytes 7962632 | tf_op jit(solution)/shard_map/ppermute | solution.py:388
  352.5 196.9 %collective-permute-start.10 = (bf16[512,768]{1,0:T(8,128)(2,1)}, bf16[512,768]{1,0:T(8,128)(2,1)}, u32[]{:S(2)}, u32[]{:S(2)}) collective-permute-start(bf16[512,768]{1,0:T(8,128)(2,1)} %get-tuple-element.39), channel_id=1, source_target_pairs={{0,1},{1,2},{2,3},{3,0},{4,5},{5,6},{6,7},{7,4},{8,9},{9,10},{10,1... | collective-permute-start | bytes 2359304 | tf_op jit(solution)/shard_map/ppermute | solution.py:383
  354.5 197.1 %collective-permute-start.11 = (bf16[512,768]{1,0:T(8,128)(2,1)}, bf16[512,768]{1,0:T(8,128)(2,1)}, u32[]{:S(2)}, u32[]{:S(2)}) collective-permute-start(bf16[512,768]{1,0:T(8,128)(2,1)} %get-tuple-element.39), channel_id=1, source_target_pairs={{0,2},{1,3},{2,0},{3,1},{4,6},{5,7},{6,4},{7,5},{8,10},{9,11},{10,... | collective-permute-start | bytes 2359304 | tf_op jit(solution)/shard_map/ppermute | solution.py:383
  354.5 78.3 %collective-permute-start.13 = (bf16[192,512]{1,0:T(8,128)(2,1)S(1)}, bf16[192,512]{1,0:T(8,128)(2,1)S(1)}, u32[]{:S(2)}, u32[]{:S(2)}) collective-permute-start(bf16[192,512]{1,0:T(8,128)(2,1)S(1)} %get-tuple-element.159), channel_id=1, source_target_pairs={{0,1},{1,2},{2,3},{3,0},{4,5},{5,6},{6,7},{7,4},{8,9},{9,10},{10,1... | collective-permute-start | bytes 589832 | tf_op jit(solution)/shard_map/ppermute | solution.py:383
  356.0 79.0 %collective-permute-start.14 = (bf16[192,512]{1,0:T(8,128)(2,1)S(1)}, bf16[192,512]{1,0:T(8,128)(2,1)S(1)}, u32[]{:S(2)}, u32[]{:S(2)}) collective-permute-start(bf16[192,512]{1,0:T(8,128)(2,1)S(1)} %get-tuple-element.158), channel_id=1, source_target_pairs={{0,2},{1,3},{2,0},{3,1},{4,6},{5,7},{6,4},{7,5},{8,10},{9,11},{10,... | collective-permute-start | bytes 589832 | tf_op jit(solution)/shard_map/ppermute | solution.py:383
  358.4 77.6 %collective-permute-start.15 = (bf16[192,512]{1,0:T(8,128)(2,1)S(1)}, bf16[192,512]{1,0:T(8,128)(2,1)S(1)}, u32[]{:S(2)}, u32[]{:S(2)}) collective-permute-start(bf16[192,512]{1,0:T(8,128)(2,1)S(1)} %get-tuple-element.157), channel_id=1, source_target_pairs={{0,3},{1,0},{2,1},{3,2},{4,7},{5,4},{6,5},{7,6},{8,11},{9,8},{10,9... | collective-permute-start | bytes 589832 | tf_op jit(solution)/shard_map/ppermute | solution.py:383
  432.9 120.8 %collective-permute-start.12 = (bf16[512,768]{1,0:T(8,128)(2,1)}, bf16[512,768]{1,0:T(8,128)(2,1)}, u32[]{:S(2)}, u32[]{:S(2)}) collective-permute-start(bf16[512,768]{1,0:T(8,128)(2,1)} %get-tuple-element.39), channel_id=1, source_target_pairs={{0,3},{1,0},{2,1},{3,2},{4,7},{5,4},{6,5},{7,6},{8,11},{9,8},{10,9... | collective-permute-start | bytes 2359304 | tf_op jit(solution)/shard_map/ppermute | solution.py:383
  435.0 197.6 %collective-permute-start.32 = (bf16[2,4,192,1728]{3,2,1,0:T(8,128)(2,1)}, bf16[2,4,192,1728]{3,2,1,0:T(8,128)(2,1)}, u32[]{:S(2)}, u32[]{:S(2)}) collective-permute-start(bf16[2,4,192,1728]{3,2,1,0:T(8,128)(2,1)} %dynamic-slice_bitcast_fusion), channel_id=1, source_target_pairs={{0,8},{8,0},{16,24},{24,16},{1,9},{9,1},{17,25},{25,17},{2,10},{10... | collective-permute-start | bytes 15925256 | tf_op jit(solution)/shard_map/ppermute | solution.py:388
  505.1 50.6 %collective-permute-start.16 = (bf16[3,128,2048]{2,1,0:T(8,128)(2,1)}, bf16[3,128,2048]{2,1,0:T(8,128)(2,1)S(1)}, u32[]{:S(2)}, u32[]{:S(2)}) collective-permute-start(bf16[3,128,2048]{2,1,0:T(8,128)(2,1)} %get-tuple-element.46), channel_id=1, source_target_pairs={{0,4},{4,0},{1,5},{5,1},{2,6},{6,2},{3,7},{7,3},{8,12},{12,8},{9,1... | collective-permute-start | bytes 4718600 | tf_op jit(solution)/shard_map/ppermute | solution.py:383
  578.1 51.0 %collective-permute-start.18 = (bf16[576,512]{1,0:T(8,128)(2,1)S(1)}, bf16[576,512]{1,0:T(8,128)(2,1)S(1)}, u32[]{:S(2)}, u32[]{:S(2)}) collective-permute-start(bf16[576,512]{1,0:T(8,128)(2,1)S(1)} %get-tuple-element.151), channel_id=1, source_target_pairs={{0,2},{1,3},{2,0},{3,1},{4,6},{5,7},{6,4},{7,5},{8,10},{9,11},{10,... | collective-permute-start | bytes 1769480 | tf_op jit(solution)/shard_map/ppermute | solution.py:383
  580.8 51.7 %collective-permute-start.19 = (bf16[576,512]{1,0:T(8,128)(2,1)S(1)}, bf16[576,512]{1,0:T(8,128)(2,1)S(1)}, u32[]{:S(2)}, u32[]{:S(2)}) collective-permute-start(bf16[576,512]{1,0:T(8,128)(2,1)S(1)} %get-tuple-element.150), channel_id=1, source_target_pairs={{0,3},{1,0},{2,1},{3,2},{4,7},{5,4},{6,5},{7,6},{8,11},{9,8},{10,9... | collective-permute-start | bytes 1769480 | tf_op jit(solution)/shard_map/ppermute | solution.py:383
  587.1 239.9 %collective-permute-start.30 = (bf16[192,576]{1,0:T(8,128)(2,1)S(1)}, bf16[192,576]{1,0:T(8,128)(2,1)}, u32[]{:S(2)}, u32[]{:S(2)}) collective-permute-start(bf16[192,576]{1,0:T(8,128)(2,1)S(1)} %dynamic-slice_bitcast_fusion.10), channel_id=1, source_target_pairs={{0,16},{8,24},{16,0},{24,8},{1,17},{9,25},{17,1},{25,9},{2,18},{10... | collective-permute-start | bytes 663560 | tf_op jit(solution)/shard_map/ppermute | solution.py:388
  642.1 193.8 %collective-permute-start.33 = (bf16[4,192,1728]{2,1,0:T(8,128)(2,1)}, bf16[4,192,1728]{2,1,0:T(8,128)(2,1)}, u32[]{:S(2)}, u32[]{:S(2)}) collective-permute-start(bf16[4,192,1728]{2,1,0:T(8,128)(2,1)} %dynamic-slice_bitcast_fusion.1), channel_id=1, source_target_pairs={{0,16},{8,24},{16,0},{24,8},{1,17},{9,25},{17,1},{25,9},{2,18},{10... | collective-permute-start | bytes 7962632 | tf_op jit(solution)/shard_map/ppermute | solution.py:388
  653.8 188.0 %collective-permute-start.26 = (bf16[512,768]{1,0:T(8,128)(2,1)}, bf16[512,768]{1,0:T(8,128)(2,1)}, u32[]{:S(2)}, u32[]{:S(2)}) collective-permute-start(bf16[512,768]{1,0:T(8,128)(2,1)} %get-tuple-element.146), channel_id=1, source_target_pairs={{0,1},{1,2},{2,3},{3,0},{4,5},{5,6},{6,7},{7,4},{8,9},{9,10},{10,1... | collective-permute-start | bytes 2359304 | tf_op jit(solution)/shard_map/ppermute | solution.py:383
  653.8 190.7 %collective-permute-start.27 = (bf16[512,768]{1,0:T(8,128)(2,1)}, bf16[512,768]{1,0:T(8,128)(2,1)}, u32[]{:S(2)}, u32[]{:S(2)}) collective-permute-start(bf16[512,768]{1,0:T(8,128)(2,1)} %get-tuple-element.146), channel_id=1, source_target_pairs={{0,2},{1,3},{2,0},{3,1},{4,6},{5,7},{6,4},{7,5},{8,10},{9,11},{10,... | collective-permute-start | bytes 2359304 | tf_op jit(solution)/shard_map/ppermute | solution.py:383
  653.9 191.9 %collective-permute-start.28 = (bf16[512,768]{1,0:T(8,128)(2,1)}, bf16[512,768]{1,0:T(8,128)(2,1)}, u32[]{:S(2)}, u32[]{:S(2)}) collective-permute-start(bf16[512,768]{1,0:T(8,128)(2,1)} %get-tuple-element.146), channel_id=1, source_target_pairs={{0,3},{1,0},{2,1},{3,2},{4,7},{5,4},{6,5},{7,6},{8,11},{9,8},{10,9... | collective-permute-start | bytes 2359304 | tf_op jit(solution)/shard_map/ppermute | solution.py:383
  839.3 46.6 %collective-permute-start.34 = (bf16[192,1728]{1,0:T(8,128)(2,1)S(1)}, bf16[192,1728]{1,0:T(8,128)(2,1)S(1)}, u32[]{:S(2)}, u32[]{:S(2)}) collective-permute-start(bf16[192,1728]{1,0:T(8,128)(2,1)S(1)} %get-tuple-element.147), channel_id=1, source_target_pairs={{0,1},{1,2},{2,3},{3,0},{4,5},{5,6},{6,7},{7,4},{8,9},{9,10},{10,1... | collective-permute-start | bytes 1990664 | tf_op jit(solution)/shard_map/ppermute | solution.py:383
  840.5 55.7 %collective-permute-start.35 = (bf16[192,1728]{1,0:T(8,128)(2,1)S(1)}, bf16[192,1728]{1,0:T(8,128)(2,1)S(1)}, u32[]{:S(2)}, u32[]{:S(2)}) collective-permute-start(bf16[192,1728]{1,0:T(8,128)(2,1)S(1)} %get-tuple-element.149), channel_id=1, source_target_pairs={{0,2},{1,3},{2,0},{3,1},{4,6},{5,7},{6,4},{7,5},{8,10},{9,11},{10,... | collective-permute-start | bytes 1990664 | tf_op jit(solution)/shard_map/ppermute | solution.py:383
  841.8 57.9 %collective-permute-start.36 = (bf16[192,1728]{1,0:T(8,128)(2,1)S(1)}, bf16[192,1728]{1,0:T(8,128)(2,1)S(1)}, u32[]{:S(2)}, u32[]{:S(2)}) collective-permute-start(bf16[192,1728]{1,0:T(8,128)(2,1)S(1)} %get-tuple-element.148), channel_id=1, source_target_pairs={{0,3},{1,0},{2,1},{3,2},{4,7},{5,4},{6,5},{7,6},{8,11},{9,8},{10,9... | collective-permute-start | bytes 1990664 | tf_op jit(solution)/shard_map/ppermute | solution.py:383
  (40 other events, 344.0 us)
Sparse Core Ops, SparseCore 0:
  648.9 171.1 all-reduce.2
